TPU v7x, 256 devices: a whole 4x4x8 slice. The times are simulated.
256 devices in a mesh: wide: 16 (over z, x_lo), narrow: 16 (over x_hi, y, core).
Axes of the slice: x: 4 (x_hi: 2, x_lo: 2; x = x_hi * 2 + x_lo), y: 4, z: 8, core: 2. Of those that a mesh axis runs over, the one named last changes fastest.
Arguments:
- panel: float32 [16, 2097152], P(None, ('wide', 'narrow'))
- signs: int32 [2097152], P(('wide', 'narrow')), may hold values from -1 to 1, as said below
- samples: int32 [16384], replicated, may hold values from 0 to 2097151, as said below
Outputs:
- mixed: float32 [16, 2097152], P(None, ('wide', 'narrow'))
- gram: float32 [16, 16], replicated
Inputs may be any that keep to these rules, and one draw needn't show every extreme that they name: `signs`: every entry is -1 or 1. `samples`: indices may repeat; the first is 0 and the last is 2097151.
All inputs are finite; a program needn't handle non-finite values.
Results may differ from a plain program's by a relative error of at most 0.000098.
Values sent between devices are 32-bit elements; how exact they have to be, the bound alone decides.
No kernel may reach another device: no remote copies, remote signals or barrier semaphores. Data moves between devices by JAX's collectives and lax.ppermute only.
A program may use at most 64 MiB of HBM per device.

v0:
```python
import jax
import jax.numpy as jnp
from jax import lax
from jax.sharding import PartitionSpec as P


def partner_2(value, axis, stride):
    mask = 2**stride
    pairs = [(source, source ^ mask) for source in range(lax.axis_size(axis))]
    return lax.ppermute(value, axis, pairs)


def hadamard(order):
    bits = order.bit_length() - 1
    first = jnp.arange(order, dtype=jnp.int32)[:, None]
    second = jnp.arange(order, dtype=jnp.int32)[None, :]
    parity = jnp.zeros((order, order), jnp.int32)
    for level in range(bits):
        parity = parity + (first >> level & 1) * (second >> level & 1)
    return jnp.where(parity % 2 == 0, 1.0, -1.0).astype(jnp.float32)


def per_device(panel, signs, samples):
    high = lax.Precision.HIGHEST
    columns, local_rows = panel.shape
    blocks = local_rows // 128
    flipped = panel * signs.astype(jnp.float32)[None, :]
    shaped = flipped.reshape(columns, blocks, 128)
    shaped = jnp.einsum("pbc,ec->pbe", shaped, hadamard(128), precision=high)
    shaped = jnp.einsum("pbc,eb->pec", shaped, hadamard(blocks), precision=high)
    current = shaped.reshape(columns, local_rows)
    narrow_count = lax.axis_size("narrow")
    wide_count = lax.axis_size("wide")
    narrow_place = lax.axis_index("narrow")
    for level in range(narrow_count.bit_length() - 1):
        partner = partner_2(current, "narrow", level)
        current = jnp.where(narrow_place >> level & 1 == 0, current + partner, partner - current)
    wide_place = lax.axis_index("wide")
    for level in range(wide_count.bit_length() - 1):
        partner = partner_2(current, "wide", level)
        current = jnp.where(wide_place >> level & 1 == 0, current + partner, partner - current)
    total_rows = local_rows * narrow_count * wide_count
    mixed = current * (1.0 / jnp.sqrt(jnp.float32(total_rows)))
    device_place = lax.axis_index("wide") * narrow_count + lax.axis_index("narrow")
    offsets = samples - device_place * local_rows
    inside = jnp.logical_and(offsets >= 0, offsets < local_rows)
    clipped = jnp.clip(offsets, 0, local_rows - 1)
    picked = jnp.take(mixed, clipped, axis=1) * inside.astype(jnp.float32)[None, :]
    partial_gram = jnp.dot(picked, picked.T, precision=high, preferred_element_type=jnp.float32)
    total_gram = lax.psum(partial_gram, ("wide", "narrow"))
    gram = total_gram / jnp.float32(samples.shape[0])
    return (mixed, gram)


def solution(mesh):
    placed = (P(None, ("wide", "narrow")), P(("wide", "narrow")), P())
    return jax.shard_map(
        per_device,
        mesh=mesh,
        in_specs=placed,
        out_specs=(P(None, ("wide", "narrow")), P()),
        check_vma=False,
    )
```

profile of v0, /device:TPU:1, one launch (start us, length us, event | category | flops | bytes accessed | tf_op | source)
XLA Modules:
  0.0 373.8 jit_solution(9968325390276020278)
XLA Ops:
  0.7 0.8 convert_element_type.6
  1.5 1.1 multiply_bitcast_fusion
  2.7 0.7 fusion.8
  3.4 0.6 fusion.18
  4.1 0.3 copy.38
  4.4 3.3 collective-permute-start
  7.7 2.6 copy.9
  10.3 2.6 copy.10
  13.0 5.9 %subtract_select_fusion.6 = f32[16,8192]{0,1:T(8,128)} fusion(f32[16,8192]{0,1:T(8,128)} %copy.10, f32[16,8192]{0,1:T(8,128)} %copy.9, pred[]{:T(512)S(6)} %eq.43), kind=kLoop, calls=%fused_computation.13 | loop fusion | flops 393216 | bytes 1572865 | tf_op jit(solution)/shard_map/jit(_where)/select_n | solution.py:37
  18.8 2.8 copy.13
  21.7 13.5 %collective-permute-done.1 = f32[16,8192]{1,0:T(8,128)S(1)} collective-permute-done((f32[16,8192]{1,0:T(8,128)S(1)}, f32[16,8192]{1,0:T(8,128)S(1)}, u32[]{:S(2)}, u32[]{:S(2)}) %collective-permute-start.1) | collective-permute-done | bytes 524320 | tf_op jit(solution)/shard_map/ppermute | solution.py:10
  35.3 2.6 copy.14
  37.9 5.8 %subtract_select_fusion.5 = f32[16,8192]{0,1:T(8,128)} fusion(f32[16,8192]{0,1:T(8,128)} %copy.14, f32[16,8192]{0,1:T(8,128)} %subtract_select_fusion.6, pred[]{:T(512)S(6)} %eq.42), kind=kLoop, calls=%fused_computation.12 | loop fusion | flops 393216 | bytes 1572865 | tf_op jit(solution)/shard_map/jit(_where)/select_n | solution.py:37
  43.7 2.8 copy.16
  46.5 1.3 collective-permute-start.2
  47.8 13.0 %collective-permute-done.2 = f32[16,8192]{1,0:T(8,128)S(1)} collective-permute-done((f32[16,8192]{1,0:T(8,128)S(1)}, f32[16,8192]{1,0:T(8,128)S(1)}, u32[]{:S(2)}, u32[]{:S(2)}) %collective-permute-start.2) | collective-permute-done | bytes 524320 | tf_op jit(solution)/shard_map/ppermute | solution.py:10
  60.7 2.6 copy.17
  63.4 5.9 %subtract_select_fusion.4 = f32[16,8192]{0,1:T(8,128)} fusion(f32[16,8192]{0,1:T(8,128)} %copy.17, f32[16,8192]{0,1:T(8,128)} %subtract_select_fusion.5, pred[]{:T(512)S(6)} %eq.41), kind=kLoop, calls=%fused_computation.11 | loop fusion | flops 393216 | bytes 1572865 | tf_op jit(solution)/shard_map/jit(_where)/select_n | solution.py:37
  69.3 2.8 copy.19
  72.0 1.1 collective-permute-start.3
  73.1 12.2 %collective-permute-done.3 = f32[16,8192]{1,0:T(8,128)S(1)} collective-permute-done((f32[16,8192]{1,0:T(8,128)S(1)}, f32[16,8192]{1,0:T(8,128)S(1)}, u32[]{:S(2)}, u32[]{:S(2)}) %collective-permute-start.3) | collective-permute-done | bytes 524320 | tf_op jit(solution)/shard_map/ppermute | solution.py:10
  85.4 2.6 copy.20
  88.0 5.8 %subtract_select_fusion.3 = f32[16,8192]{0,1:T(8,128)} fusion(f32[16,8192]{0,1:T(8,128)} %copy.20, f32[16,8192]{0,1:T(8,128)} %subtract_select_fusion.4, pred[]{:T(512)S(6)} %eq.40), kind=kLoop, calls=%fused_computation.10 | loop fusion | flops 393216 | bytes 1572865 | tf_op jit(solution)/shard_map/jit(_where)/select_n | solution.py:37
  93.8 2.8 copy.22
  96.7 10.8 %collective-permute-done.4 = f32[16,8192]{1,0:T(8,128)S(1)} collective-permute-done((f32[16,8192]{1,0:T(8,128)S(1)}, f32[16,8192]{1,0:T(8,128)S(1)}, u32[]{:S(2)}, u32[]{:S(2)}) %collective-permute-start.4) | collective-permute-done | bytes 524320 | tf_op jit(solution)/shard_map/ppermute | solution.py:10
  107.5 2.6 copy.23
  110.1 5.9 %subtract_select_fusion.2 = f32[16,8192]{0,1:T(8,128)} fusion(f32[16,8192]{0,1:T(8,128)} %copy.23, f32[16,8192]{0,1:T(8,128)} %subtract_select_fusion.3, pred[]{:T(512)S(6)} %eq.39), kind=kLoop, calls=%fused_computation.9 | loop fusion | flops 393216 | bytes 1572865 | tf_op jit(solution)/shard_map/jit(_where)/select_n | solution.py:41
  116.0 2.8 copy.25
  118.8 0.3 collective-permute-start.5
  119.1 9.9 %collective-permute-done.5 = f32[16,8192]{1,0:T(8,128)S(1)} collective-permute-done((f32[16,8192]{1,0:T(8,128)S(1)}, f32[16,8192]{1,0:T(8,128)S(1)}, u32[]{:S(2)}, u32[]{:S(2)}) %collective-permute-start.5) | collective-permute-done | bytes 524320 | tf_op jit(solution)/shard_map/ppermute | solution.py:10
  129.0 2.6 copy.26
  131.6 5.8 %subtract_select_fusion.1 = f32[16,8192]{0,1:T(8,128)} fusion(f32[16,8192]{0,1:T(8,128)} %copy.26, f32[16,8192]{0,1:T(8,128)} %subtract_select_fusion.2, pred[]{:T(512)S(6)} %eq.38), kind=kLoop, calls=%fused_computation.8 | loop fusion | flops 393216 | bytes 1572865 | tf_op jit(solution)/shard_map/jit(_where)/select_n | solution.py:41
  137.4 2.8 copy.28
  140.2 1.7 collective-permute-start.6
  141.9 24.1 %collective-permute-done.6 = f32[16,8192]{1,0:T(8,128)S(1)} collective-permute-done((f32[16,8192]{1,0:T(8,128)S(1)}, f32[16,8192]{1,0:T(8,128)S(1)}, u32[]{:S(2)}, u32[]{:S(2)}) %collective-permute-start.6) | collective-permute-done | bytes 524320 | tf_op jit(solution)/shard_map/ppermute | solution.py:10
  166.0 2.6 copy.29
  168.7 5.9 %subtract_select_fusion = f32[16,8192]{0,1:T(8,128)} fusion(f32[16,8192]{0,1:T(8,128)} %copy.29, f32[16,8192]{0,1:T(8,128)} %subtract_select_fusion.1, pred[]{:T(512)S(6)} %eq.37), kind=kLoop, calls=%fused_computation.7 | loop fusion | flops 393216 | bytes 1572865 | tf_op jit(solution)/shard_map/jit(_where)/select_n | solution.py:41
  174.5 2.8 copy.31
  177.3 5.0 %collective-permute-start.7 = (f32[16,8192]{1,0:T(8,128)S(1)}, f32[16,8192]{1,0:T(8,128)S(1)}, u32[]{:S(2)}, u32[]{:S(2)}) collective-permute-start(f32[16,8192]{1,0:T(8,128)S(1)} %copy.31), channel_id=1, source_target_pairs={{0,128},{16,144},{32,160},{48,176},{64,192},{80,208},{96,224},{112... | collective-permute-start | bytes 1572872 | tf_op jit(solution)/shard_map/ppermute | solution.py:10
  182.4 22.9 %collective-permute-done.7 = f32[16,8192]{1,0:T(8,128)S(1)} collective-permute-done((f32[16,8192]{1,0:T(8,128)S(1)}, f32[16,8192]{1,0:T(8,128)S(1)}, u32[]{:S(2)}, u32[]{:S(2)}) %collective-permute-start.7) | collective-permute-done | bytes 524320 | tf_op jit(solution)/shard_map/ppermute | solution.py:10
  205.4 2.6 copy.32
  208.0 6.0 %select_multiply_fusion = f32[16,8192]{0,1:T(8,128)} fusion(f32[16,8192]{0,1:T(8,128)} %copy.32, f32[16,8192]{0,1:T(8,128)} %subtract_select_fusion, pred[]{:T(512)S(6)} %eq.36), kind=kLoop, calls=%fused_computation.6 | loop fusion | flops 524288 | bytes 1572865 | tf_op jit(solution)/shard_map/mul | solution.py:43
  214.0 3.5 copy.34
  217.5 56.6 %gather_fusion = f32[16384,16]{1,0:T(8,128)} fusion(f32[16,8192]{0,1:T(8,128)} %select_multiply_fusion, s32[16384]{0:T(1024)S(1)} %fusion.15), kind=kCustom, calls=%fused_computation | custom fusion | bytes 2162688 | tf_op jit(solution)/shard_map/jit(_take)/gather | solution.py:48
  274.1 6.7 %fusion.78 = f32[16384,16]{1,0:T(8,128)S(1)} fusion(f32[16384,16]{1,0:T(8,128)} %gather_fusion, f32[16384]{0:T(1024)S(1)} %get-tuple-element.7, pred[16384]{0:T(1024)(128)(4,1)S(1)} %get-tuple-element.6), kind=kLoop, calls=%fused_computation.2.clone.2 | loop fusion | flops 524288 | bytes 2179072 | tf_op jit(solution)/shard_map/dot_general | solution.py:49
  280.8 14.3 %fusion = f32[16,16]{1,0:T(8,128)S(1)} fusion(f32[16384,16]{1,0:T(8,128)S(1)} %fusion.78), kind=kOutput, calls=%fused_computation.1 | convolution fusion | flops 50331648 | bytes 1049600 | tf_op jit(solution)/shard_map/dot_general | solution.py:49
  295.1 78.1 %psum.7 = f32[16,16]{1,0:T(8,128)S(1)} all-reduce(f32[16,16]{1,0:T(8,128)S(1)} %fusion), channel_id=1, replica_groups=mesh['wide'=16,'narrow'=16] {'wide','narrow'}, use_global_device_ids=true, to_apply=%region_0.1 | all-reduce | flops 256 | bytes 2048 | tf_op jit(solution)/shard_map/psum | solution.py:50
  373.2 0.6 broadcast_multiply_fusion
  (15 shorter events, 0.4 us)
Async XLA Ops:
  4.4 5.9 %collective-permute-start = (f32[16,8192]{1,0:T(8,128)S(1)}, f32[16,8192]{1,0:T(8,128)S(1)}, u32[]{:S(2)}, u32[]{:S(2)}) collective-permute-start(f32[16,8192]{1,0:T(8,128)S(1)} %bitcast.17), channel_id=1, source_target_pairs={{0,1},{1,0},{2,3},{3,2},{4,5},{5,4},{6,7},{7,6},{8,9},{9,8},{10,11... | collective-permute-start | bytes 1572872 | tf_op jit(solution)/shard_map/ppermute | solution.py:10
  21.6 13.6 %collective-permute-start.1 = (f32[16,8192]{1,0:T(8,128)S(1)}, f32[16,8192]{1,0:T(8,128)S(1)}, u32[]{:S(2)}, u32[]{:S(2)}) collective-permute-start(f32[16,8192]{1,0:T(8,128)S(1)} %copy.13), channel_id=1, source_target_pairs={{0,2},{1,3},{2,0},{3,1},{4,6},{5,7},{6,4},{7,5},{8,10},{9,11},{10,... | collective-permute-start | bytes 1572872 | tf_op jit(solution)/shard_map/ppermute | solution.py:10
  46.5 14.2 %collective-permute-start.2 = (f32[16,8192]{1,0:T(8,128)S(1)}, f32[16,8192]{1,0:T(8,128)S(1)}, u32[]{:S(2)}, u32[]{:S(2)}) collective-permute-start(f32[16,8192]{1,0:T(8,128)S(1)} %copy.16), channel_id=1, source_target_pairs={{0,4},{1,5},{2,6},{3,7},{4,0},{5,1},{6,2},{7,3},{8,12},{9,13},{10,... | collective-permute-start | bytes 1572872 | tf_op jit(solution)/shard_map/ppermute | solution.py:10
  72.0 13.3 %collective-permute-start.3 = (f32[16,8192]{1,0:T(8,128)S(1)}, f32[16,8192]{1,0:T(8,128)S(1)}, u32[]{:S(2)}, u32[]{:S(2)}) collective-permute-start(f32[16,8192]{1,0:T(8,128)S(1)} %copy.19), channel_id=1, source_target_pairs={{0,8},{1,9},{2,10},{3,11},{4,12},{5,13},{6,14},{7,15},{8,0},{9,1},... | collective-permute-start | bytes 1572872 | tf_op jit(solution)/shard_map/ppermute | solution.py:10
  96.6 10.9 %collective-permute-start.4 = (f32[16,8192]{1,0:T(8,128)S(1)}, f32[16,8192]{1,0:T(8,128)S(1)}, u32[]{:S(2)}, u32[]{:S(2)}) collective-permute-start(f32[16,8192]{1,0:T(8,128)S(1)} %copy.22), channel_id=1, source_target_pairs={{0,16},{16,0},{32,48},{48,32},{64,80},{80,64},{96,112},{112,96},{1... | collective-permute-start | bytes 1572872 | tf_op jit(solution)/shard_map/ppermute | solution.py:10
  118.8 10.2 %collective-permute-start.5 = (f32[16,8192]{1,0:T(8,128)S(1)}, f32[16,8192]{1,0:T(8,128)S(1)}, u32[]{:S(2)}, u32[]{:S(2)}) collective-permute-start(f32[16,8192]{1,0:T(8,128)S(1)} %copy.25), channel_id=1, source_target_pairs={{0,32},{16,48},{32,0},{48,16},{64,96},{80,112},{96,64},{112,80},{1... | collective-permute-start | bytes 1572872 | tf_op jit(solution)/shard_map/ppermute | solution.py:10
  140.2 25.8 %collective-permute-start.6 = (f32[16,8192]{1,0:T(8,128)S(1)}, f32[16,8192]{1,0:T(8,128)S(1)}, u32[]{:S(2)}, u32[]{:S(2)}) collective-permute-start(f32[16,8192]{1,0:T(8,128)S(1)} %copy.28), channel_id=1, source_target_pairs={{0,64},{16,80},{32,96},{48,112},{64,0},{80,16},{96,32},{112,48},{1... | collective-permute-start | bytes 1572872 | tf_op jit(solution)/shard_map/ppermute | solution.py:10
  174.5 7.8 %copy-start = (s32[16384]{0:T(1024)S(1)}, s32[16384]{0:T(1024)}, u32[]{:S(2)}) copy-start(s32[16384]{0:T(1024)} %param.5) | copy-start | bytes 196612
  177.3 28.0 %collective-permute-start.7 = (f32[16,8192]{1,0:T(8,128)S(1)}, f32[16,8192]{1,0:T(8,128)S(1)}, u32[]{:S(2)}, u32[]{:S(2)}) collective-permute-start(f32[16,8192]{1,0:T(8,128)S(1)} %copy.31), channel_id=1, source_target_pairs={{0,128},{16,144},{32,160},{48,176},{64,192},{80,208},{96,224},{112... | collective-permute-start | bytes 1572872 | tf_op jit(solution)/shard_map/ppermute | solution.py:10
where the time goes:
time: 374 us
  waiting for transfers between devices  106 us (28%)
  local copies, waits for them, and re-layouts  104 us (28%)
  blocking collectives  78.1 us (21%)
  other arithmetic  56.2 us (15%)
  matrix products  15.7 us (4%)
  starting transfers between devices  12.8 us (3%)
    ppermute x8, waiting for transfers between devices, partner_2(): return lax.ppermute(value, axis, pairs)  106 us
    psum x1, blocking collectives, per_device(): total_gram = lax.psum(partial_gram, ('wide', 'narrow'))  78.1 us
    gather x1, local copies, waits for them, and re-layouts, per_device(): jnp.take(mixed, clipped, axis=1) * inside.astype(jnp.float32)[None, :]  56.6 us
    select_n x4, other arithmetic, per_device(): jnp.where(narrow_place >> level & 1 == 0, current + partner, partner - cu...  23.4 us
    ppermute x8, local copies, waits for them, and re-layouts, partner_2(): return lax.ppermute(value, axis, pairs)  21 us
    select_n x3, other arithmetic, per_device(): jnp.where(wide_place >> level & 1 == 0, current + partner, partner - curr...  17.6 us
    dot_general x1, matrix products, per_device(): jnp.dot(picked, picked.T, precision=high, preferred_element_type=jnp.floa...  14.3 us
    ppermute x8, starting transfers between devices, partner_2(): return lax.ppermute(value, axis, pairs)  12.8 us
  transfers between devices with their start and end apart: 8, of which 7 were waited for; matrix products, arithmetic and copies ran while one was open for 1% of the time, Pallas kernels for 0%

commit v1 on v0

v1 whole, which is shorter than its diff:
```python
import functools

import jax
import jax.numpy as jnp
from jax import lax
from jax.experimental import pallas as pl
from jax.experimental.pallas import tpu as pltpu
from jax.sharding import PartitionSpec as P

COLUMNS = 16
LANES = 128
BLOCKS = 64
DEVICES = 256
LOCAL_ROWS = BLOCKS * LANES
SAMPLES = 16384
BOTH = ("wide", "narrow")
NT = (((1,), (1,)), ((), ()))
HIGH = lax.Precision.HIGHEST
VMEM = pl.BlockSpec(memory_space=pltpu.VMEM)
SMEM = pl.BlockSpec(memory_space=pltpu.SMEM)
LIMIT = 32 * 1024 * 1024


def hadamard(rows, columns):
    first = lax.broadcasted_iota(jnp.int32, (rows, columns), 0)
    second = lax.broadcasted_iota(jnp.int32, (rows, columns), 1)
    bits = first & second
    bits = bits ^ (bits >> 4)
    bits = bits ^ (bits >> 2)
    bits = bits ^ (bits >> 1)
    return jnp.where((bits & 1) == 0, 1.0, -1.0).astype(jnp.bfloat16)


def split(value):
    high = value.astype(jnp.bfloat16)
    low = (value - high.astype(jnp.float32)).astype(jnp.bfloat16)
    return high, low


def butterfly(parts):
    step = 1
    while step < len(parts):
        parts = [
            parts[i] + parts[i + step] if i & step == 0 else parts[i - step] - parts[i]
            for i in range(len(parts))
        ]
        step *= 2
    return parts


def local_kernel(panel_ref, signs_ref, out_ref):
    signs = signs_ref[...].astype(jnp.float32)
    parts = [
        panel_ref[:, b * LANES : (b + 1) * LANES] * signs[b : b + 1, :] for b in range(BLOCKS)
    ]
    parts = butterfly(parts)
    had = hadamard(LANES, LANES)
    twice = jnp.concatenate([had, had], axis=1)
    for group in range(8):
        block = jnp.concatenate(parts[8 * group : 8 * group + 8], axis=0)
        pair = jnp.concatenate(split(block), axis=1)
        done = lax.dot_general(twice, pair, NT, preferred_element_type=jnp.float32)
        out_ref[pl.ds(group, LANES, stride=8), :] = done


def count_kernel(place_ref, samples_ref, count_ref, had_ref):
    place = place_ref[0]
    lane, top = place >> 1, place & 1
    wide_rows = 8
    count_ref[...] = jnp.zeros_like(count_ref)

    def body(step, carry):
        rows = samples_ref[pl.ds(step * wide_rows, wide_rows), :]
        owners, blocks = [], []
        for r in range(wide_rows):
            row = rows[r : r + 1, :]
            mine = jnp.logical_and((row & 127) == lane, ((row >> 12) & 1) == top)
            block = jnp.where(mine, (row >> 7) & 31, -1)
            owner = row >> 13
            owners.append(lax.broadcasted_iota(jnp.int32, (DEVICES, LANES), 0) == owner)
            blocks.append(lax.broadcasted_iota(jnp.int32, (32, LANES), 0) == block)
        hot = lambda masks: jnp.concatenate(
            [jnp.where(m, 1.0, 0.0).astype(jnp.bfloat16) for m in masks], axis=1
        )
        count_ref[...] += lax.dot_general(
            hot(blocks), hot(owners), NT, preferred_element_type=jnp.float32
        )
        return carry

    lax.fori_loop(0, SAMPLES // (wide_rows * LANES), body, 0)
    had_ref[...] = hadamard(DEVICES, DEVICES)


def across_kernel(parts_ref, count_ref, had_ref, out_ref):
    scale = 1.0 / jnp.sqrt(jnp.float32(DEVICES * LOCAL_ROWS))
    had = had_ref[...]
    columns = []
    for group in range(4):
        high, low = split(parts_ref[pl.ds(group, DEVICES, stride=4), :])
        done = jnp.dot(had, high, preferred_element_type=jnp.float32)
        done = (done + jnp.dot(had, low, preferred_element_type=jnp.float32)) * scale
        out_ref[pl.ds(group, DEVICES, stride=5), :] = done
        turned = done.T
        columns += [turned[16 * b : 16 * b + 16, :] for b in range(8)]
    counts = count_ref[...]
    weighed = [column * counts[b : b + 1, :] for b, column in enumerate(columns)]
    gram = lax.dot_general(
        jnp.concatenate(weighed, axis=1),
        jnp.concatenate(columns, axis=1),
        NT,
        precision=HIGH,
        preferred_element_type=jnp.float32,
    )
    lanes = lax.broadcasted_iota(jnp.int32, (COLUMNS, LANES), 1)
    rows = lax.broadcasted_iota(jnp.int32, (COLUMNS, LANES), 0)
    tile = jnp.where((lanes & 15) == rows, 1.0, 0.0)
    tiled = jnp.dot(gram, tile, precision=HIGH, preferred_element_type=jnp.float32)
    kept = jnp.where((lanes >> 4) == (rows & 7), tiled, 0.0)
    upper = jnp.sum(kept[:8, :], axis=0, keepdims=True)
    lower = jnp.sum(kept[8:, :], axis=0, keepdims=True)
    core = lax.broadcasted_iota(jnp.int32, (DEVICES, LANES), 0) & 1
    out_ref[pl.ds(4, DEVICES, stride=5), :] = jnp.where(
        core == 0, jnp.broadcast_to(upper, core.shape), jnp.broadcast_to(lower, core.shape)
    )


def gather_kernel(parts_ref, gram_ref):
    rows = parts_ref[pl.ds(4, DEVICES, stride=5), :]
    gram_ref[...] = jnp.sum(rows, axis=0, keepdims=True)


def place_kernel(parts_ref, out_ref):
    for top in range(2):
        for group in range(4):
            turned = parts_ref[pl.ds(top * 5 + group, LANES, stride=10), :].T
            for b in range(8):
                block = top * 32 + group * 8 + b
                out_ref[:, block * LANES : (block + 1) * LANES] = turned[16 * b : 16 * b + 16, :]


def call(kernel, outs, operands, name, specs=None, flops=0, size=1 << 20):
    return pl.pallas_call(
        kernel,
        out_shape=outs,
        in_specs=specs or [VMEM] * len(operands),
        out_specs=jax.tree.map(lambda _: VMEM, outs),
        compiler_params=pltpu.CompilerParams(vmem_limit_bytes=LIMIT),
        cost_estimate=pl.CostEstimate(flops=flops, bytes_accessed=size, transcendentals=0),
        name=name,
    )(*operands)


def per_device(panel, signs, samples):
    shape = jax.ShapeDtypeStruct
    f32 = jnp.float32
    narrow_count = lax.axis_size("narrow")
    place = lax.axis_index("wide") * narrow_count + lax.axis_index("narrow")
    parts = call(
        local_kernel,
        shape((1024, LANES), f32),
        (panel, signs.reshape(BLOCKS, LANES)),
        "local_transform",
    )
    arrived = lax.all_to_all(parts.reshape(DEVICES, 4, LANES), BOTH, 0, 0, tiled=True)
    counts, had = call(
        count_kernel,
        (shape((32, DEVICES), f32), shape((DEVICES, DEVICES), jnp.bfloat16)),
        (place.reshape(1).astype(jnp.int32), samples.reshape(LANES, LANES)),
        "count_samples",
        specs=[SMEM, VMEM],
        flops=1 << 30,
    )
    mixed_parts = call(
        across_kernel,
        shape((DEVICES * 5, LANES), f32),
        (arrived.reshape(1024, LANES), counts, had),
        "across_devices",
    )
    back = lax.all_to_all(mixed_parts.reshape(DEVICES, 1, 5 * LANES), BOTH, 0, 0, tiled=True)
    back = back.reshape(DEVICES * 5, LANES)
    half = call(gather_kernel, shape((1, LANES), f32), (back,), "sum_gram")
    other = lax.ppermute(half, "narrow", [(s, s ^ 1) for s in range(narrow_count)])
    mixed = call(place_kernel, shape((COLUMNS, LOCAL_ROWS), f32), (back,), "place_rows")
    even = place & 1 == 0
    upper = jnp.where(even, half, other).reshape(8, COLUMNS)
    lower = jnp.where(even, other, half).reshape(8, COLUMNS)
    gram = jnp.concatenate([upper, lower], axis=0) / jnp.float32(SAMPLES)
    return (mixed, gram)


def solution(mesh):
    placed = (P(None, BOTH), P(BOTH), P())
    return jax.shard_map(
        per_device,
        mesh=mesh,
        in_specs=placed,
        out_specs=(P(None, BOTH), P()),
        check_vma=False,
    )
```

time: 374 us -> 75.4 us (0.20)
  local copies, waits for them, and re-layouts: 104 us -> 1.95 us
  waiting for transfers between devices: 106 us -> 16.4 us
  other arithmetic: 56.2 us -> 0.63 us
  blocking collectives: 78.1 us -> 29.8 us
  matrix products: 15.7 us -> 0 us
  Pallas kernels: 0 us -> 8.86 us
  starting transfers between devices: 12.8 us -> 16.8 us
    ppermute x8 -> x1, waiting for transfers between devices: 106 us -> 0.01 us  [per_device(): lax.ppermute(half, 'narrow', [(s, s ^ 1) for s in range(narrow_count)])]
    psum x1 -> x0, blocking collectives: 78.1 us -> none  [per_device(): total_gram = lax.psum(partial_gram, ('wide', 'narrow'))]
    gather x1 -> x0, local copies, waits for them, and re-layouts: 56.6 us -> none  [per_device(): jnp.take(mixed, clipped, axis=1) * inside.astype(jnp.float32)[None, :]]
    select_n x7 -> x1, other arithmetic: 41 us -> 0.02 us  [per_device(): upper = jnp.where(even, half, other).reshape(8, COLUMNS)]
    all_to_all x0 -> x1, blocking collectives: none -> 29.8 us  [per_device(): lax.all_to_all(mixed_parts.reshape(DEVICES, 1, 5 * LANES), BOTH, 0, 0, ti...]
    ppermute x8 -> x0, local copies, waits for them, and re-layouts: 21 us -> none  [partner_2(): return lax.ppermute(value, axis, pairs)]
    select_n x7 -> x0, local copies, waits for them, and re-layouts: 19.5 us -> none  [the longest x4 11.1 us: per_device(): jnp.where(narrow_place >> level & 1 == 0, current + partner, partner - cu...]
    all_to_all x0 -> x1, waiting for transfers between devices: none -> 16.4 us  [per_device(): lax.all_to_all(parts.reshape(DEVICES, 4, LANES), BOTH, 0, 0, tiled=True)]
  transfers between devices with their start and end apart: 8 -> 2, of which waited for: 7 -> 1; matrix products, arithmetic and copies ran while one was open for 1% -> 0% of each run, Pallas kernels for 0% -> 8%
where the time goes in v1:
time: 75.4 us; the launch traced here: 75.1 us
  blocking collectives  29.8 us (40%)
  starting transfers between devices  16.8 us (22%)
  waiting for transfers between devices  16.4 us (22%)
  Pallas kernels  8.86 us (12%)
  local copies, waits for them, and re-layouts  1.95 us (3%)
    all_to_all x1, blocking collectives, per_device(): lax.all_to_all(mixed_parts.reshape(DEVICES, 1, 5 * LANES), BOTH, 0, 0, ti...  29.8 us
    all_to_all x1, waiting for transfers between devices, per_device(): lax.all_to_all(parts.reshape(DEVICES, 4, LANES), BOTH, 0, 0, tiled=True)  16.4 us
    all_to_all x1, starting transfers between devices, per_device(): lax.all_to_all(parts.reshape(DEVICES, 4, LANES), BOTH, 0, 0, tiled=True)  15.7 us
    pallas_call x5, Pallas kernels, call(): pl.pallas_call(kernel, out_shape=outs, in_specs=specs or [VMEM] * len(ope...  8.86 us
    unnamed x6, local copies, waits for them, and re-layouts  1.8 us
  transfers between devices with their start and end apart: 2, of which 1 were waited for; matrix products, arithmetic and copies ran while one was open for 0% of the time, Pallas kernels for 8%

profile of v1, /device:TPU:1, one launch (start us, length us, event | category | flops | bytes accessed | tf_op | source)
XLA Modules:
  0.0 75.1 jit_solution(1635797336367001639)
XLA Ops:
  0.6 0.0 copy-start
  0.6 1.0 %copy-done = f32[16,8192]{1,0:T(8,128)S(1)} copy-done((f32[16,8192]{1,0:T(8,128)S(1)}, f32[16,8192]{1,0:T(8,128)}, u32[]{:S(2)}) %copy-start) | copy-done | bytes 524312
  1.7 0.0 copy-start.1
  1.7 0.8 %copy-done.1 = s32[8192]{0:T(1024)S(1)} copy-done((s32[8192]{0:T(1024)S(1)}, s32[8192]{0:T(1024)}, u32[]{:S(2)}) %copy-start.1) | copy-done | bytes 32792
  2.4 1.3 %local_transform.1 = f32[1024,128]{1,0:T(8,128)} custom-call(f32[16,8192]{1,0:T(8,128)S(1)} %copy-done, s32[64,128]{1,0:T(8,128)S(1)} %bitcast.11), custom_call_target="tpu_custom_call" | custom-call | bytes 1048576 | tf_op jit(solution)/shard_map/local_transform/pallas_call | solution.py:142
  3.7 0.0 copy-start.2
  3.7 15.7 %all-to-all-start = ((f32[256,4,128]{2,1,0:T(4,128)}), f32[256,4,128]{2,1,0:T(4,128)S(1)}, u32[]{:S(2)}, u32[]{:S(2)}) async-start(f32[256,4,128]{2,1,0:T(4,128)} %bitcast.1), calls=%async_computation | async-start | bytes 1048576 | tf_op jit(solution)/shard_map/all_to_all | solution.py:164
  19.4 0.0 copy-done.2
  19.4 4.8 %count_samples.1 = (f32[32,256]{1,0:T(8,128)S(1)}, bf16[256,256]{1,0:T(8,128)(2,1)S(1)}) custom-call(s32[1]{0:T(128)} %bitcast.3.place_ref, s32[128,128]{1,0:T(8,128)S(1)} %bitcast.12), custom_call_target="tpu_custom_call" | custom-call | flops 1073741824 | bytes 1048576 | tf_op jit(solution)/shard_map/count_samples/pallas_call | solution.py:142
  24.2 16.4 %all-to-all-done = f32[256,4,128]{2,1,0:T(4,128)S(1)} async-done(((f32[256,4,128]{2,1,0:T(4,128)}), f32[256,4,128]{2,1,0:T(4,128)S(1)}, u32[]{:S(2)}, u32[]{:S(2)}) %all-to-all-start) | async-done | bytes 524320 | tf_op jit(solution)/shard_map/all_to_all | solution.py:164
  40.5 1.8 %across_devices.1 = f32[1280,128]{1,0:T(8,128)S(1)} custom-call(f32[1024,128]{1,0:T(8,128)S(1)} %bitcast.10, f32[32,256]{1,0:T(8,128)S(1)} %get-tuple-element.4.count_ref, bf16[256,256]{1,0:T(8,128)(2,1)S(1)} %get-tuple-element.5.had_ref), custom_call_target="tpu_custom_call" | custom-call | bytes 1048576 | tf_op jit(solution)/shard_map/across_devices/pallas_call | solution.py:142
  42.3 29.8 %all_to_all.10 = f32[256,1,640]{2,1,0:T(1,128)S(1)} all-to-all(f32[256,1,640]{2,1,0:T(1,128)S(1)} %bitcast.9), channel_id=1, replica_groups=mesh['wide'=16,'narrow'=16] {'wide','narrow'}, dimensions={0} | all-to-all | bytes 1310720 | tf_op jit(solution)/shard_map/all_to_all | solution.py:179
  72.1 1.2 %collective-permute-start = (f32[1,128]{1,0:T(1,128)S(1)}, f32[1,128]{1,0:T(1,128)S(1)}, u32[]{:S(2)}, u32[]{:S(2)}) collective-permute-start(f32[1,128]{1,0:T(1,128)S(1)} %sum_gram.1), channel_id=1, source_target_pairs={{0,1},{1,0},{2,3},{3,2},{4,5},{5,4},{6,7},{7,6},{8,9},{9,8},{10,11... | collective-permute-start | bytes 1544 | tf_op jit(solution)/shard_map/ppermute | solution.py:182
  73.3 1.0 %place_rows.1 = f32[16,8192]{1,0:T(8,128)} custom-call(f32[1280,128]{1,0:T(8,128)S(1)} %bitcast.8), custom_call_target="tpu_custom_call" | custom-call | bytes 1048576 | tf_op jit(solution)/shard_map/place_rows/pallas_call | solution.py:142
  74.3 0.0 collective-permute-done
  74.3 0.1 reshape.38
  74.4 0.1 reshape.39
  74.5 0.6 maximum_multiply_fusion
  (2 shorter events, 0.1 us)
Async XLA Ops:
  0.6 1.0 %copy-start = (f32[16,8192]{1,0:T(8,128)S(1)}, f32[16,8192]{1,0:T(8,128)}, u32[]{:S(2)}) copy-start(f32[16,8192]{1,0:T(8,128)} %panel_ref.1) | copy-start | bytes 1572868
  1.7 0.8 %copy-start.1 = (s32[8192]{0:T(1024)S(1)}, s32[8192]{0:T(1024)}, u32[]{:S(2)}) copy-start(s32[8192]{0:T(1024)} %param.4) | copy-start | bytes 98308
  3.7 15.7 %copy-start.2 = (s32[16384]{0:T(1024)S(1)}, s32[16384]{0:T(1024)}, u32[]{:S(2)}) copy-start(s32[16384]{0:T(1024)} %param.5) | copy-start | bytes 196612
  3.7 36.8 %all-to-all-start = ((f32[256,4,128]{2,1,0:T(4,128)}), f32[256,4,128]{2,1,0:T(4,128)S(1)}, u32[]{:S(2)}, u32[]{:S(2)}) async-start(f32[256,4,128]{2,1,0:T(4,128)} %bitcast.1), calls=%async_computation | async-start | bytes 1048576 | tf_op jit(solution)/shard_map/all_to_all | solution.py:164
  72.1 2.2 %collective-permute-start = (f32[1,128]{1,0:T(1,128)S(1)}, f32[1,128]{1,0:T(1,128)S(1)}, u32[]{:S(2)}, u32[]{:S(2)}) collective-permute-start(f32[1,128]{1,0:T(1,128)S(1)} %sum_gram.1), channel_id=1, source_target_pairs={{0,1},{1,0},{2,3},{3,2},{4,5},{5,4},{6,7},{7,6},{8,9},{9,8},{10,11... | collective-permute-start | bytes 1544 | tf_op jit(solution)/shard_map/ppermute | solution.py:182

commit v2 on v1

v2 whole, which is shorter than its diff:
```python
import jax
import jax.numpy as jnp
from jax import lax
from jax.experimental import pallas as pl
from jax.experimental.pallas import tpu as pltpu
from jax.sharding import Mesh
from jax.sharding import PartitionSpec as P

COLUMNS = 16
LANES = 128
BLOCKS = 64
CHIPS = 128
LOCAL_ROWS = BLOCKS * LANES
ROWS = 2 * CHIPS * LOCAL_ROWS
SAMPLES = 16384
WIDTH = 10
CHIP_AXES = ("wide", "slow")
ALL_AXES = ("wide", "slow", "core")
NT = (((1,), (1,)), ((), ()))
HIGH = lax.Precision.HIGHEST
VMEM = pl.BlockSpec(memory_space=pltpu.VMEM)
SMEM = pl.BlockSpec(memory_space=pltpu.SMEM)
HBM = pl.BlockSpec(memory_space=pltpu.HBM)
LIMIT = 32 * 1024 * 1024


def hadamard_twice():
    first = lax.broadcasted_iota(jnp.int32, (LANES, LANES), 0)
    second = lax.broadcasted_iota(jnp.int32, (LANES, LANES), 1)
    bits = first & second
    bits = bits ^ (bits >> 4)
    bits = bits ^ (bits >> 2)
    bits = bits ^ (bits >> 1)
    had = jnp.where((bits & 1) == 0, 1.0, -1.0).astype(jnp.bfloat16)
    return jnp.concatenate([had, had], axis=1)


def split(value):
    high = value.astype(jnp.bfloat16)
    low = (value - high.astype(jnp.float32)).astype(jnp.bfloat16)
    return high, low


def butterfly(parts):
    step = 1
    while step < len(parts):
        parts = [
            parts[i] + parts[i + step] if i & step == 0 else parts[i - step] - parts[i]
            for i in range(len(parts))
        ]
        step *= 2
    return parts


def local_kernel(panel_hbm, signs_hbm, out_ref, panel_ref, signs_ref, panel_sem, signs_sem):
    halves = [
        pltpu.make_async_copy(
            panel_hbm.at[pl.ds(8 * half, 8), :], panel_ref.at[half], panel_sem.at[half]
        )
        for half in range(2)
    ]
    signs_copy = pltpu.make_async_copy(signs_hbm, signs_ref, signs_sem)
    signs_copy.start()
    for half in halves:
        half.start()
    twice = hadamard_twice()
    signs_copy.wait()
    for half in range(2):
        halves[half].wait()
        signs = signs_ref[...].astype(jnp.float32)
        parts = [
            panel_ref[half, :, b * LANES : (b + 1) * LANES] * signs[b : b + 1, :]
            for b in range(BLOCKS)
        ]
        parts = butterfly(parts)
        for quarter in range(4):
            block = jnp.concatenate(parts[16 * quarter : 16 * quarter + 16], axis=0)
            pair = jnp.concatenate(split(block), axis=1)
            done = lax.dot_general(twice, pair, NT, preferred_element_type=jnp.float32)
            out_ref[pl.ds(4 * half + quarter, LANES, stride=8), :] = done


def count_kernel(chip_ref, samples_ref, count_ref):
    chip = chip_ref[0]
    wide_rows = 8
    count_ref[...] = jnp.zeros_like(count_ref)

    def body(step, carry):
        rows = samples_ref[pl.ds(step * wide_rows, wide_rows), :]
        owners, places = [], []
        for r in range(wide_rows):
            row = rows[r : r + 1, :]
            place = ((row >> 13) & 1) * BLOCKS + ((row >> 7) & 63)
            place = jnp.where((row & 127) == chip, place, -1)
            owner = row >> 14
            index = lax.broadcasted_iota(jnp.int32, (CHIPS, LANES), 0)
            owners.append(jnp.where(index == owner, 1.0, 0.0).astype(jnp.bfloat16))
            places.append(jnp.where(index == place, 1.0, 0.0).astype(jnp.bfloat16))
        count_ref[...] += lax.dot_general(
            jnp.concatenate(places, axis=1),
            jnp.concatenate(owners, axis=1),
            NT,
            preferred_element_type=jnp.float32,
        )
        return carry

    lax.fori_loop(0, SAMPLES // (wide_rows * LANES), body, 0)


def chips_transform(parts_ref, group, twice):
    pair = jnp.concatenate(split(parts_ref[pl.ds(group, CHIPS, stride=8), :]), axis=0)
    return jnp.dot(twice, pair, preferred_element_type=jnp.float32)


def own_kernel(parts_ref, out_ref, turned_ref):
    twice = hadamard_twice()
    for group in range(8):
        done = chips_transform(parts_ref, group, twice)
        rows = slice(group * CHIPS, (group + 1) * CHIPS)
        out_ref[rows, :] = done
        turned_ref[rows, :] = done.T


def both_kernel(core_ref, parts_ref, own_ref, turned_ref, count_ref, out_ref):
    scale = 1.0 / jnp.sqrt(jnp.float32(ROWS))
    side = (1 - 2 * core_ref[0]).astype(jnp.float32) * scale
    twice = hadamard_twice()
    sums, gaps = [], []
    for group in range(8):
        done = chips_transform(parts_ref, group, twice)
        rows = slice(group * CHIPS, (group + 1) * CHIPS)
        out_ref[pl.ds(group, CHIPS, stride=WIDTH), :] = done * scale + own_ref[rows, :] * side
        other, own = done.T, turned_ref[rows, :]
        sums.append((own + other) * scale)
        gaps.append((own - other) * scale)
    columns = []
    for turned in (sums, gaps):
        for b in range(BLOCKS):
            rows = slice(8 * (b % 16), 8 * (b % 16) + 8)
            columns.append(
                jnp.concatenate([turned[b // 16][rows, :], turned[4 + b // 16][rows, :]], axis=0)
            )
    counts = count_ref[...]
    weighed = [column * counts[b : b + 1, :] for b, column in enumerate(columns)]
    weighed = jnp.concatenate(split(jnp.concatenate(weighed, axis=1)), axis=0)
    columns = jnp.concatenate(split(jnp.concatenate(columns, axis=1)), axis=0)
    gram = lax.dot_general(weighed, columns, NT, preferred_element_type=jnp.float32)
    gram = gram[:, :COLUMNS] + gram[:, COLUMNS:]
    gram = gram[:COLUMNS, :] + gram[COLUMNS:, :]
    lanes = lax.broadcasted_iota(jnp.int32, (COLUMNS, LANES), 1)
    rows = lax.broadcasted_iota(jnp.int32, (COLUMNS, LANES), 0)
    tile = jnp.where((lanes & 15) == rows, 1.0, 0.0)
    tiled = jnp.dot(gram, tile, precision=HIGH, preferred_element_type=jnp.float32)
    kept = jnp.where((lanes >> 4) == (rows & 7), tiled, 0.0)
    for half in range(2):
        flat = jnp.sum(kept[8 * half : 8 * half + 8, :], axis=0, keepdims=True)
        out_ref[pl.ds(8 + half, CHIPS, stride=WIDTH), :] = jnp.broadcast_to(flat, (CHIPS, LANES))


def place_kernel(parts_ref, out_ref, gram_ref):
    for half in range(2):
        for quarter in range(4):
            turned = parts_ref[pl.ds(4 * half + quarter, LANES, stride=WIDTH), :].T
            for b in range(16):
                block = quarter * 16 + b
                out_ref[8 * half : 8 * half + 8, block * LANES : (block + 1) * LANES] = turned[
                    8 * b : 8 * b + 8, :
                ]
    lanes = lax.broadcasted_iota(jnp.int32, (8, LANES), 1)
    rows = lax.broadcasted_iota(jnp.int32, (8, LANES), 0)
    pick = jnp.where(
        (lax.broadcasted_iota(jnp.int32, (LANES, COLUMNS), 0) & 15)
        == lax.broadcasted_iota(jnp.int32, (LANES, COLUMNS), 1),
        1.0,
        0.0,
    )
    for half in range(2):
        flat = jnp.sum(
            parts_ref[pl.ds(8 + half, CHIPS, stride=WIDTH), :], axis=0, keepdims=True
        )
        spread = jnp.where((lanes >> 4) == rows, jnp.broadcast_to(flat, (8, LANES)), 0.0)
        block = jnp.dot(spread, pick, precision=HIGH, preferred_element_type=jnp.float32)
        gram_ref[8 * half : 8 * half + 8, :] = block / jnp.float32(SAMPLES)


def call(kernel, outs, operands, name, specs=None, scratch=(), flops=0, limit=LIMIT):
    return pl.pallas_call(
        kernel,
        out_shape=outs,
        in_specs=specs or [VMEM] * len(operands),
        out_specs=jax.tree.map(lambda _: VMEM, outs),
        scratch_shapes=scratch,
        compiler_params=pltpu.CompilerParams(vmem_limit_bytes=limit),
        cost_estimate=pl.CostEstimate(flops=flops, bytes_accessed=1 << 20, transcendentals=0),
        name=name,
    )(*operands)


def per_device(panel, signs, samples):
    f32 = jnp.float32
    whole = jax.ShapeDtypeStruct((1024, LANES), f32)
    core = lax.axis_index("core").astype(jnp.int32).reshape(1)
    chip = lax.axis_index("wide") * lax.axis_size("slow") + lax.axis_index("slow")
    chip = chip.astype(jnp.int32).reshape(1)
    exchange = lambda value: lax.all_to_all(value, CHIP_AXES, 0, 0, tiled=True)
    parts = call(
        local_kernel,
        whole,
        (panel, signs.reshape(BLOCKS, LANES)),
        "local_transform",
        specs=[HBM, HBM],
        scratch=[
            pltpu.VMEM((2, 8, LOCAL_ROWS), f32),
            pltpu.VMEM((BLOCKS, LANES), jnp.int32),
            pltpu.SemaphoreType.DMA((2,)),
            pltpu.SemaphoreType.DMA(()),
        ],
        limit=60 * 1024 * 1024,
    )
    parts = exchange(parts.reshape(CHIPS, 8, LANES)).reshape(1024, LANES)
    counts = call(
        count_kernel,
        jax.ShapeDtypeStruct((2 * BLOCKS, CHIPS), f32),
        (chip, samples.reshape(LANES, LANES)),
        "count_samples",
        specs=[SMEM, VMEM],
        flops=1 << 30,
    )
    parts, counts = lax.optimization_barrier((parts, counts))
    other = lax.ppermute(parts, "core", [(0, 1), (1, 0)])
    own, turned = call(own_kernel, (whole, whole), (parts,), "own_chips_transform", flops=1 << 28)
    back = call(
        both_kernel,
        jax.ShapeDtypeStruct((CHIPS * WIDTH, LANES), f32),
        (core, other, own, turned, counts),
        "both_cores",
        specs=[SMEM] + [VMEM] * 4,
    )
    back = exchange(back.reshape(CHIPS, 1, WIDTH * LANES)).reshape(CHIPS * WIDTH, LANES)
    return call(
        place_kernel,
        (
            jax.ShapeDtypeStruct((COLUMNS, LOCAL_ROWS), f32),
            jax.ShapeDtypeStruct((COLUMNS, COLUMNS), f32),
        ),
        (back,),
        "place_rows",
    )


def solution(mesh):
    wide, narrow = mesh.devices.shape
    split_mesh = Mesh(mesh.devices.reshape(wide, narrow // 2, 2), ALL_AXES)
    return jax.shard_map(
        per_device,
        mesh=split_mesh,
        in_specs=(P(None, ALL_AXES), P(ALL_AXES), P()),
        out_specs=(P(None, ALL_AXES), P()),
        check_vma=False,
    )
```

time: 75.4 us -> 71.2 us (0.944)
  blocking collectives: 29.8 us -> 26.9 us
  waiting for transfers between devices: 16.4 us -> 13.5 us
  starting transfers between devices: 16.8 us -> 19.4 us
  local copies, waits for them, and re-layouts: 1.95 us -> 0.01 us
  Pallas kernels: 8.86 us -> 9.76 us
    all_to_all x1, waiting for transfers between devices: 16.4 us -> 12.4 us  [per_device(): exchange = lambda value: lax.all_to_all(value, CHIP_AXES, 0, 0, tiled=True)]
    all_to_all x1, blocking collectives: 29.8 us -> 26.9 us  [per_device(): exchange = lambda value: lax.all_to_all(value, CHIP_AXES, 0, 0, tiled=True)]
    unnamed x6 -> x2, local copies, waits for them, and re-layouts: 1.8 us -> 0.01 us
    ppermute x1, starting transfers between devices: 1.18 us -> 2.96 us  [per_device(): other = lax.ppermute(parts, 'core', [(0, 1), (1, 0)])]
    ppermute x1, waiting for transfers between devices: 0.01 us -> 1.14 us  [per_device(): other = lax.ppermute(parts, 'core', [(0, 1), (1, 0)])]
    pallas_call x5, Pallas kernels: 8.86 us -> 9.76 us  [call(): pl.pallas_call(kernel, out_shape=outs, in_specs=specs or [VMEM] * len(ope...]
    all_to_all x1, starting transfers between devices: 15.7 us -> 16.5 us  [per_device(): exchange = lambda value: lax.all_to_all(value, CHIP_AXES, 0, 0, tiled=True)]
  transfers between devices with their start and end apart: 2 -> 2, of which waited for: 1 -> 2; matrix products, arithmetic and copies ran while one was open for 0% -> 0% of each run, Pallas kernels for 8% -> 7%
where the time goes in v2:
time: 71.2 us; the launch traced here: 70.3 us
  blocking collectives  26.9 us (38%)
  starting transfers between devices  19.4 us (27%)
  waiting for transfers between devices  13.5 us (19%)
  Pallas kernels  9.76 us (14%)
    all_to_all x1, blocking collectives, per_device(): exchange = lambda value: lax.all_to_all(value, CHIP_AXES, 0, 0, tiled=True)  26.9 us
    all_to_all x1, starting transfers between devices, per_device(): exchange = lambda value: lax.all_to_all(value, CHIP_AXES, 0, 0, tiled=True)  16.5 us
    all_to_all x1, waiting for transfers between devices, per_device(): exchange = lambda value: lax.all_to_all(value, CHIP_AXES, 0, 0, tiled=True)  12.4 us
    pallas_call x5, Pallas kernels, call(): pl.pallas_call(kernel, out_shape=outs, in_specs=specs or [VMEM] * len(ope...  9.76 us
    ppermute x1, starting transfers between devices, per_device(): other = lax.ppermute(parts, 'core', [(0, 1), (1, 0)])  2.96 us
  transfers between devices with their start and end apart: 2, of which 2 were waited for; matrix products, arithmetic and copies ran while one was open for 0% of the time, Pallas kernels for 7%

profile of v2, /device:TPU:1, one launch (start us, length us, event | category | flops | bytes accessed | tf_op | source)
XLA Modules:
  0.0 70.3 jit_solution(2786941560061896591)
XLA Ops:
  0.6 2.4 %local_transform.1 = f32[1024,128]{1,0:T(8,128)} custom-call(f32[16,8192]{1,0:T(8,128)} %panel_hbm.1, s32[64,128]{1,0:T(8,128)} %bitcast.14), custom_call_target="tpu_custom_call" | custom-call | bytes 1048576 | tf_op jit(solution)/shard_map/local_transform/pallas_call | solution.py:187
  3.0 0.0 copy-start
  3.0 16.5 %all-to-all-start = ((f32[128,8,128]{2,1,0:T(8,128)}), f32[128,8,128]{2,1,0:T(8,128)S(1)}, u32[]{:S(2)}, u32[]{:S(2)}) async-start(f32[128,8,128]{2,1,0:T(8,128)} %bitcast.13), calls=%async_computation | async-start | bytes 1048576 | tf_op jit(solution)/shard_map/all_to_all | solution.py:205
  19.5 0.0 copy-done
  19.5 4.8 %count_samples.1.count_ref = f32[128,128]{1,0:T(8,128)S(1)} custom-call(s32[1]{0:T(128)} %bitcast.4.chip_ref, s32[128,128]{1,0:T(8,128)S(1)} %bitcast.12), custom_call_target="tpu_custom_call" | custom-call | flops 1073741824 | bytes 1048576 | tf_op jit(solution)/shard_map/count_samples/pallas_call | solution.py:187
  24.3 12.4 %all-to-all-done = f32[128,8,128]{2,1,0:T(8,128)S(1)} async-done(((f32[128,8,128]{2,1,0:T(8,128)}), f32[128,8,128]{2,1,0:T(8,128)S(1)}, u32[]{:S(2)}, u32[]{:S(2)}) %all-to-all-start) | async-done | bytes 524320 | tf_op jit(solution)/shard_map/all_to_all | solution.py:205
  36.7 3.0 %collective-permute-start = (f32[1024,128]{1,0:T(8,128)S(1)}, f32[1024,128]{1,0:T(8,128)S(1)}, u32[]{:S(2)}, u32[]{:S(2)}) collective-permute-start(f32[1024,128]{1,0:T(8,128)S(1)} %bitcast.10), channel_id=1, source_target_pairs={{0,1},{1,0},{2,3},{3,2},{4,5},{5,4},{6,7},{7,6},{8,9},{9,8},{10,11... | collective-permute-start | bytes 1572872 | tf_op jit(solution)/shard_map/ppermute | solution.py:230
  39.6 0.4 own_chips_transform.1
  40.0 1.1 %collective-permute-done.parts_ref = f32[1024,128]{1,0:T(8,128)S(1)} collective-permute-done((f32[1024,128]{1,0:T(8,128)S(1)}, f32[1024,128]{1,0:T(8,128)S(1)}, u32[]{:S(2)}, u32[]{:S(2)}) %collective-permute-start) | collective-permute-done | bytes 524320 | tf_op jit(solution)/shard_map/ppermute | solution.py:230
  41.2 1.3 %both_cores.1 = f32[1280,128]{1,0:T(8,128)S(1)} custom-call(s32[1]{0:T(128)} %bitcast.core_ref, f32[1024,128]{1,0:T(8,128)S(1)} %collective-permute-done.parts_ref, f32[1024,128]{1,0:T(8,128)S(1)} %get-tuple-element.7.own_ref, f32[1024,128]{1,0:T(8,128)S(1)} %get-tuple-element.8.turned_ref, f32[128,128]{1,0:T(8,128)S(1)} %count_samples.1.count_ref), custom_call_target="tpu_custom_call" | custom-call | bytes 1048576 | tf_op jit(solution)/shard_map/both_cores/pallas_call | solution.py:187
  42.4 26.9 %all_to_all.10 = f32[128,1,1280]{2,1,0:T(1,128)S(1)} all-to-all(f32[128,1,1280]{2,1,0:T(1,128)S(1)} %bitcast.8), channel_id=1, replica_groups=mesh['wide'=16,'slow'=8,'core'=2] {'wide','slow'}, dimensions={0} | all-to-all | bytes 1310720 | tf_op jit(solution)/shard_map/all_to_all | solution.py:205
  69.3 1.0 %place_rows.1 = (f32[16,8192]{1,0:T(8,128)}, f32[16,16]{1,0:T(8,128)}) custom-call(f32[1280,128]{1,0:T(8,128)S(1)} %bitcast.9), custom_call_target="tpu_custom_call" | custom-call | bytes 1048576 | tf_op jit(solution)/shard_map/place_rows/pallas_call | solution.py:187
Async XLA Ops:
  3.0 16.5 %copy-start = (s32[16384]{0:T(1024)S(1)}, s32[16384]{0:T(1024)}, u32[]{:S(2)}) copy-start(s32[16384]{0:T(1024)} %param.5) | copy-start | bytes 196612
  3.0 33.6 %all-to-all-start = ((f32[128,8,128]{2,1,0:T(8,128)}), f32[128,8,128]{2,1,0:T(8,128)S(1)}, u32[]{:S(2)}, u32[]{:S(2)}) async-start(f32[128,8,128]{2,1,0:T(8,128)} %bitcast.13), calls=%async_computation | async-start | bytes 1048576 | tf_op jit(solution)/shard_map/all_to_all | solution.py:205
  36.7 4.5 %collective-permute-start = (f32[1024,128]{1,0:T(8,128)S(1)}, f32[1024,128]{1,0:T(8,128)S(1)}, u32[]{:S(2)}, u32[]{:S(2)}) collective-permute-start(f32[1024,128]{1,0:T(8,128)S(1)} %bitcast.10), channel_id=1, source_target_pairs={{0,1},{1,0},{2,3},{3,2},{4,5},{5,4},{6,7},{7,6},{8,9},{9,8},{10,11... | collective-permute-start | bytes 1572872 | tf_op jit(solution)/shard_map/ppermute | solution.py:230

commit v3 on v2

--- a/solution.py
+++ b/solution.py
@@ -19,7 +19,6 @@
 NT = (((1,), (1,)), ((), ()))
 HIGH = lax.Precision.HIGHEST
 VMEM = pl.BlockSpec(memory_space=pltpu.VMEM)
-SMEM = pl.BlockSpec(memory_space=pltpu.SMEM)
 HBM = pl.BlockSpec(memory_space=pltpu.HBM)
 LIMIT = 32 * 1024 * 1024
 
@@ -52,24 +51,18 @@
     return parts
 
 
-def local_kernel(panel_hbm, signs_hbm, out_ref, panel_ref, signs_ref, panel_sem, signs_sem):
-    halves = [
-        pltpu.make_async_copy(
-            panel_hbm.at[pl.ds(8 * half, 8), :], panel_ref.at[half], panel_sem.at[half]
-        )
-        for half in range(2)
-    ]
-    signs_copy = pltpu.make_async_copy(signs_hbm, signs_ref, signs_sem)
-    signs_copy.start()
-    for half in halves:
-        half.start()
+def bring_kernel(panel_hbm, panel_ref, sem):
+    copy = pltpu.make_async_copy(panel_hbm, panel_ref, sem)
+    copy.start()
+    copy.wait()
+
+
+def local_kernel(panel_ref, signs_ref, out_ref):
     twice = hadamard_twice()
-    signs_copy.wait()
-    for half in range(2):
-        halves[half].wait()
-        signs = signs_ref[...].astype(jnp.float32)
+    signs = signs_ref[...].astype(jnp.float32)
+    for half in range(2):
         parts = [
-            panel_ref[half, :, b * LANES : (b + 1) * LANES] * signs[b : b + 1, :]
+            panel_ref[8 * half : 8 * half + 8, b * LANES : (b + 1) * LANES] * signs[b : b + 1, :]
             for b in range(BLOCKS)
         ]
         parts = butterfly(parts)
@@ -80,31 +73,26 @@
             out_ref[pl.ds(4 * half + quarter, LANES, stride=8), :] = done
 
 
-def count_kernel(chip_ref, samples_ref, count_ref):
-    chip = chip_ref[0]
-    wide_rows = 8
-    count_ref[...] = jnp.zeros_like(count_ref)
-
-    def body(step, carry):
-        rows = samples_ref[pl.ds(step * wide_rows, wide_rows), :]
-        owners, places = [], []
-        for r in range(wide_rows):
-            row = rows[r : r + 1, :]
-            place = ((row >> 13) & 1) * BLOCKS + ((row >> 7) & 63)
-            place = jnp.where((row & 127) == chip, place, -1)
-            owner = row >> 14
-            index = lax.broadcasted_iota(jnp.int32, (CHIPS, LANES), 0)
-            owners.append(jnp.where(index == owner, 1.0, 0.0).astype(jnp.bfloat16))
-            places.append(jnp.where(index == place, 1.0, 0.0).astype(jnp.bfloat16))
-        count_ref[...] += lax.dot_general(
-            jnp.concatenate(places, axis=1),
-            jnp.concatenate(owners, axis=1),
-            NT,
-            preferred_element_type=jnp.float32,
-        )
-        return carry
-
-    lax.fori_loop(0, SAMPLES // (wide_rows * LANES), body, 0)
+def count_kernel(samples_ref, count_ref):
+    chip = lax.axis_index("wide") * lax.axis_size("slow") + lax.axis_index("slow")
+    rows = samples_ref[...]
+    place = ((rows >> 13) & 1) * BLOCKS + ((rows >> 7) & 63)
+    place = jnp.where((rows & 127) == chip, place, -1).astype(jnp.float32)
+    owner = (rows >> 14).astype(jnp.float32)
+    index = lax.broadcasted_iota(jnp.int32, (CHIPS, LANES), 0)
+    index = index.astype(jnp.float32).astype(jnp.bfloat16)
+    one, zero = jnp.ones_like(index), jnp.zeros_like(index)
+
+    def hot(values):
+        spread = [
+            jnp.broadcast_to(values[r : r + 1, :], index.shape).astype(jnp.bfloat16)
+            for r in range(SAMPLES // LANES)
+        ]
+        return jnp.concatenate([jnp.where(index == row, one, zero) for row in spread], axis=1)
+
+    count_ref[...] = lax.dot_general(
+        hot(place), hot(owner), NT, preferred_element_type=jnp.float32
+    )
 
 
 def chips_transform(parts_ref, group, twice):
@@ -113,26 +101,28 @@
 
 
 def own_kernel(parts_ref, out_ref, turned_ref):
+    scale = 1.0 / jnp.sqrt(jnp.float32(ROWS))
     twice = hadamard_twice()
     for group in range(8):
         done = chips_transform(parts_ref, group, twice)
         rows = slice(group * CHIPS, (group + 1) * CHIPS)
+        done = done * scale
         out_ref[rows, :] = done
         turned_ref[rows, :] = done.T
 
 
-def both_kernel(core_ref, parts_ref, own_ref, turned_ref, count_ref, out_ref):
+def both_kernel(parts_ref, own_ref, turned_ref, count_ref, out_ref):
     scale = 1.0 / jnp.sqrt(jnp.float32(ROWS))
-    side = (1 - 2 * core_ref[0]).astype(jnp.float32) * scale
+    side = (1 - 2 * lax.axis_index("core")).astype(jnp.float32)
     twice = hadamard_twice()
     sums, gaps = [], []
     for group in range(8):
-        done = chips_transform(parts_ref, group, twice)
+        done = chips_transform(parts_ref, group, twice) * scale
         rows = slice(group * CHIPS, (group + 1) * CHIPS)
-        out_ref[pl.ds(group, CHIPS, stride=WIDTH), :] = done * scale + own_ref[rows, :] * side
+        out_ref[pl.ds(group, CHIPS, stride=WIDTH), :] = done + own_ref[rows, :] * side
         other, own = done.T, turned_ref[rows, :]
-        sums.append((own + other) * scale)
-        gaps.append((own - other) * scale)
+        sums.append(own + other)
+        gaps.append(own - other)
     columns = []
     for turned in (sums, gaps):
         for b in range(BLOCKS):
@@ -199,42 +189,33 @@
 def per_device(panel, signs, samples):
     f32 = jnp.float32
     whole = jax.ShapeDtypeStruct((1024, LANES), f32)
-    core = lax.axis_index("core").astype(jnp.int32).reshape(1)
-    chip = lax.axis_index("wide") * lax.axis_size("slow") + lax.axis_index("slow")
-    chip = chip.astype(jnp.int32).reshape(1)
     exchange = lambda value: lax.all_to_all(value, CHIP_AXES, 0, 0, tiled=True)
-    parts = call(
-        local_kernel,
-        whole,
-        (panel, signs.reshape(BLOCKS, LANES)),
-        "local_transform",
-        specs=[HBM, HBM],
-        scratch=[
-            pltpu.VMEM((2, 8, LOCAL_ROWS), f32),
-            pltpu.VMEM((BLOCKS, LANES), jnp.int32),
-            pltpu.SemaphoreType.DMA((2,)),
-            pltpu.SemaphoreType.DMA(()),
-        ],
-        limit=60 * 1024 * 1024,
-    )
+    panel = call(
+        bring_kernel,
+        jax.ShapeDtypeStruct((COLUMNS, LOCAL_ROWS), f32),
+        (panel,),
+        "bring_panel",
+        specs=[HBM],
+        scratch=[pltpu.SemaphoreType.DMA(())],
+        limit=53 * 1024 * 1024,
+    )
+    parts = call(local_kernel, whole, (panel, signs.reshape(BLOCKS, LANES)), "local_transform")
     parts = exchange(parts.reshape(CHIPS, 8, LANES)).reshape(1024, LANES)
+    parts, samples = lax.optimization_barrier((parts, samples))
+    other = lax.ppermute(parts, "core", [(0, 1), (1, 0)])
+    own, turned = call(own_kernel, (whole, whole), (parts,), "own_chips_transform", flops=1 << 28)
     counts = call(
         count_kernel,
         jax.ShapeDtypeStruct((2 * BLOCKS, CHIPS), f32),
-        (chip, samples.reshape(LANES, LANES)),
+        (samples.reshape(LANES, LANES),),
         "count_samples",
-        specs=[SMEM, VMEM],
         flops=1 << 30,
     )
-    parts, counts = lax.optimization_barrier((parts, counts))
-    other = lax.ppermute(parts, "core", [(0, 1), (1, 0)])
-    own, turned = call(own_kernel, (whole, whole), (parts,), "own_chips_transform", flops=1 << 28)
     back = call(
         both_kernel,
         jax.ShapeDtypeStruct((CHIPS * WIDTH, LANES), f32),
-        (core, other, own, turned, counts),
+        (other, own, turned, counts),
         "both_cores",
-        specs=[SMEM] + [VMEM] * 4,
     )
     back = exchange(back.reshape(CHIPS, 1, WIDTH * LANES)).reshape(CHIPS * WIDTH, LANES)
     return call(

time: 71.2 us -> 70.2 us (0.986)
  blocking collectives: 26.9 us -> 59.9 us
  starting transfers between devices: 19.4 us -> 2.96 us
  waiting for transfers between devices: 13.5 us -> 0.01 us
  Pallas kernels: 9.76 us -> 5.41 us
    all_to_all x1 -> x2, blocking collectives: 26.9 us -> 59.9 us  [per_device(): exchange = lambda value: lax.all_to_all(value, CHIP_AXES, 0, 0, tiled=True)]
    all_to_all x1 -> x0, starting transfers between devices: 16.5 us -> none  [per_device(): exchange = lambda value: lax.all_to_all(value, CHIP_AXES, 0, 0, tiled=True)]
    all_to_all x1 -> x0, waiting for transfers between devices: 12.4 us -> none  [per_device(): exchange = lambda value: lax.all_to_all(value, CHIP_AXES, 0, 0, tiled=True)]
    pallas_call x5 -> x6, Pallas kernels: 9.76 us -> 5.41 us  [call(): pl.pallas_call(kernel, out_shape=outs, in_specs=specs or [VMEM] * len(ope...]
    ppermute x1, waiting for transfers between devices: 1.14 us -> 0.01 us  [per_device(): other = lax.ppermute(parts, 'core', [(0, 1), (1, 0)])]
  transfers between devices with their start and end apart: 2 -> 1, of which waited for: 2 -> 0; matrix products, arithmetic and copies ran while one was open for 0% -> 0% of each run, Pallas kernels for 7% -> 2%
where the time goes in v3:
time: 70.2 us; the launch traced here: 69 us
  blocking collectives  59.9 us (85%)
  Pallas kernels  5.41 us (8%)
  starting transfers between devices  2.96 us (4%)
    all_to_all x2, blocking collectives, per_device(): exchange = lambda value: lax.all_to_all(value, CHIP_AXES, 0, 0, tiled=True)  59.9 us
    pallas_call x6, Pallas kernels, call(): pl.pallas_call(kernel, out_shape=outs, in_specs=specs or [VMEM] * len(ope...  5.41 us
    ppermute x1, starting transfers between devices, per_device(): other = lax.ppermute(parts, 'core', [(0, 1), (1, 0)])  2.96 us
  transfers between devices with their start and end apart: 1, of which 0 were waited for; matrix products, arithmetic and copies ran while one was open for 0% of the time, Pallas kernels for 2%

profile of v3, /device:TPU:1, one launch (start us, length us, event | category | flops | bytes accessed | tf_op | source)
XLA Modules:
  0.0 69.0 jit_solution(994419252282170923)
XLA Ops:
  0.6 0.0 copy-start
  0.6 1.1 %bring_panel.1.panel_ref = f32[16,8192]{1,0:T(8,128)S(1)} custom-call(f32[16,8192]{1,0:T(8,128)} %panel_hbm.1), custom_call_target="tpu_custom_call" | custom-call | bytes 1048576 | tf_op jit(solution)/shard_map/bring_panel/pallas_call | solution.py:177
  1.7 0.0 copy-done
  1.7 0.5 local_transform.1
  2.2 33.3 %all_to_all.10 = f32[128,8,128]{2,1,0:T(8,128)S(1)} all-to-all(f32[128,8,128]{2,1,0:T(8,128)S(1)} %bitcast.8), channel_id=1, replica_groups=mesh['wide'=16,'slow'=8,'core'=2] {'wide','slow'}, dimensions={0} | all-to-all | bytes 1048576 | tf_op jit(solution)/shard_map/all_to_all | solution.py:192
  35.5 0.0 copy-start.1
  35.5 3.0 %collective-permute-start = (f32[1024,128]{1,0:T(8,128)S(1)}, f32[1024,128]{1,0:T(8,128)S(1)}, u32[]{:S(2)}, u32[]{:S(2)}) collective-permute-start(f32[1024,128]{1,0:T(8,128)S(1)} %bitcast.9), channel_id=1, source_target_pairs={{0,1},{1,0},{2,3},{3,2},{4,5},{5,4},{6,7},{7,6},{8,9},{9,8},{10,11... | collective-permute-start | bytes 1572872 | tf_op jit(solution)/shard_map/ppermute | solution.py:205
  38.4 0.4 own_chips_transform.1
  38.8 0.0 copy-done.1
  38.9 1.2 %count_samples.1.count_ref = f32[128,128]{1,0:T(8,128)S(1)} custom-call(s32[128,128]{1,0:T(8,128)S(1)} %bitcast.12), custom_call_target="tpu_custom_call" | custom-call | flops 1073741824 | bytes 1048576 | tf_op jit(solution)/shard_map/count_samples/pallas_call | solution.py:177
  40.1 0.0 collective-permute-done.parts_ref
  40.1 1.2 %both_cores.1 = f32[1280,128]{1,0:T(8,128)S(1)} custom-call(f32[1024,128]{1,0:T(8,128)S(1)} %collective-permute-done.parts_ref, f32[1024,128]{1,0:T(8,128)S(1)} %get-tuple-element.7.own_ref, f32[1024,128]{1,0:T(8,128)S(1)} %get-tuple-element.8.turned_ref, f32[128,128]{1,0:T(8,128)S(1)} %count_samples.1.count_ref), custom_call_target="tpu_custom_call" | custom-call | bytes 1048576 | tf_op jit(solution)/shard_map/both_cores/pallas_call | solution.py:177
  41.4 26.6 %all_to_all.11 = f32[128,1,1280]{2,1,0:T(1,128)S(1)} all-to-all(f32[128,1,1280]{2,1,0:T(1,128)S(1)} %bitcast.7), channel_id=1, replica_groups=mesh['wide'=16,'slow'=8,'core'=2] {'wide','slow'}, dimensions={0} | all-to-all | bytes 1310720 | tf_op jit(solution)/shard_map/all_to_all | solution.py:192
  68.0 1.0 %place_rows.1 = (f32[16,8192]{1,0:T(8,128)}, f32[16,16]{1,0:T(8,128)}) custom-call(f32[1280,128]{1,0:T(8,128)S(1)} %bitcast.6), custom_call_target="tpu_custom_call" | custom-call | bytes 1048576 | tf_op jit(solution)/shard_map/place_rows/pallas_call | solution.py:177
Async XLA Ops:
  0.6 1.1 %copy-start = (s32[8192]{0:T(1024)S(1)}, s32[8192]{0:T(1024)}, u32[]{:S(2)}) copy-start(s32[8192]{0:T(1024)} %param.4) | copy-start | bytes 98308
  35.5 3.4 %copy-start.1 = (s32[16384]{0:T(1024)S(1)}, s32[16384]{0:T(1024)}, u32[]{:S(2)}) copy-start(s32[16384]{0:T(1024)} %param.5) | copy-start | bytes 196612
  35.5 4.6 %collective-permute-start = (f32[1024,128]{1,0:T(8,128)S(1)}, f32[1024,128]{1,0:T(8,128)S(1)}, u32[]{:S(2)}, u32[]{:S(2)}) collective-permute-start(f32[1024,128]{1,0:T(8,128)S(1)} %bitcast.9), channel_id=1, source_target_pairs={{0,1},{1,0},{2,3},{3,2},{4,5},{5,4},{6,7},{7,6},{8,9},{9,8},{10,11... | collective-permute-start | bytes 1572872 | tf_op jit(solution)/shard_map/ppermute | solution.py:205

commit v4 on v3

--- a/solution.py
+++ b/solution.py
@@ -51,18 +51,28 @@
     return parts
 
 
-def bring_kernel(panel_hbm, panel_ref, sem):
-    copy = pltpu.make_async_copy(panel_hbm, panel_ref, sem)
-    copy.start()
-    copy.wait()
-
-
-def local_kernel(panel_ref, signs_ref, out_ref):
+def local_kernel(
+    panel_hbm, signs_hbm, samples_hbm, out_ref, samples_ref, panel_ref, signs_ref, sems
+):
+    signs_copy = pltpu.make_async_copy(signs_hbm, signs_ref, sems.at[2])
+    signs_copy.start()
+    halves = []
+    for half in range(2):
+        halves.append(
+            pltpu.make_async_copy(
+                panel_hbm.at[pl.ds(8 * half, 8), :], panel_ref.at[half], sems.at[half]
+            )
+        )
+        halves[half].start()
+    samples_copy = pltpu.make_async_copy(samples_hbm, samples_ref, sems.at[3])
+    samples_copy.start()
     twice = hadamard_twice()
-    signs = signs_ref[...].astype(jnp.float32)
-    for half in range(2):
+    signs_copy.wait()
+    for half in range(2):
+        halves[half].wait()
+        signs = signs_ref[...].astype(jnp.float32)
         parts = [
-            panel_ref[8 * half : 8 * half + 8, b * LANES : (b + 1) * LANES] * signs[b : b + 1, :]
+            panel_ref[half, :, b * LANES : (b + 1) * LANES] * signs[b : b + 1, :]
             for b in range(BLOCKS)
         ]
         parts = butterfly(parts)
@@ -71,6 +81,7 @@
             pair = jnp.concatenate(split(block), axis=1)
             done = lax.dot_general(twice, pair, NT, preferred_element_type=jnp.float32)
             out_ref[pl.ds(4 * half + quarter, LANES, stride=8), :] = done
+    samples_copy.wait()
 
 
 def count_kernel(samples_ref, count_ref):
@@ -147,15 +158,7 @@
         out_ref[pl.ds(8 + half, CHIPS, stride=WIDTH), :] = jnp.broadcast_to(flat, (CHIPS, LANES))
 
 
-def place_kernel(parts_ref, out_ref, gram_ref):
-    for half in range(2):
-        for quarter in range(4):
-            turned = parts_ref[pl.ds(4 * half + quarter, LANES, stride=WIDTH), :].T
-            for b in range(16):
-                block = quarter * 16 + b
-                out_ref[8 * half : 8 * half + 8, block * LANES : (block + 1) * LANES] = turned[
-                    8 * b : 8 * b + 8, :
-                ]
+def place_kernel(parts_ref, out_hbm, gram_hbm, out_ref, gram_ref, sems):
     lanes = lax.broadcasted_iota(jnp.int32, (8, LANES), 1)
     rows = lax.broadcasted_iota(jnp.int32, (8, LANES), 0)
     pick = jnp.where(
@@ -164,21 +167,39 @@
         1.0,
         0.0,
     )
-    for half in range(2):
+    copies = []
+    for half in range(2):
+        for quarter in range(4):
+            turned = parts_ref[pl.ds(4 * half + quarter, LANES, stride=WIDTH), :].T
+            for b in range(16):
+                block = quarter * 16 + b
+                out_ref[half, :, block * LANES : (block + 1) * LANES] = turned[
+                    8 * b : 8 * b + 8, :
+                ]
+        copies.append(
+            pltpu.make_async_copy(
+                out_ref.at[half], out_hbm.at[pl.ds(8 * half, 8), :], sems.at[half]
+            )
+        )
+        copies[half].start()
         flat = jnp.sum(
             parts_ref[pl.ds(8 + half, CHIPS, stride=WIDTH), :], axis=0, keepdims=True
         )
         spread = jnp.where((lanes >> 4) == rows, jnp.broadcast_to(flat, (8, LANES)), 0.0)
         block = jnp.dot(spread, pick, precision=HIGH, preferred_element_type=jnp.float32)
         gram_ref[8 * half : 8 * half + 8, :] = block / jnp.float32(SAMPLES)
-
-
-def call(kernel, outs, operands, name, specs=None, scratch=(), flops=0, limit=LIMIT):
+    copies.append(pltpu.make_async_copy(gram_ref, gram_hbm, sems.at[2]))
+    copies[2].start()
+    for copy in copies:
+        copy.wait()
+
+
+def call(kernel, outs, operands, name, specs=None, out_specs=None, scratch=(), flops=0, limit=LIMIT):
     return pl.pallas_call(
         kernel,
         out_shape=outs,
         in_specs=specs or [VMEM] * len(operands),
-        out_specs=jax.tree.map(lambda _: VMEM, outs),
+        out_specs=out_specs or jax.tree.map(lambda _: VMEM, outs),
         scratch_shapes=scratch,
         compiler_params=pltpu.CompilerParams(vmem_limit_bytes=limit),
         cost_estimate=pl.CostEstimate(flops=flops, bytes_accessed=1 << 20, transcendentals=0),
@@ -190,16 +211,23 @@
     f32 = jnp.float32
     whole = jax.ShapeDtypeStruct((1024, LANES), f32)
     exchange = lambda value: lax.all_to_all(value, CHIP_AXES, 0, 0, tiled=True)
-    panel = call(
-        bring_kernel,
-        jax.ShapeDtypeStruct((COLUMNS, LOCAL_ROWS), f32),
-        (panel,),
-        "bring_panel",
-        specs=[HBM],
-        scratch=[pltpu.SemaphoreType.DMA(())],
-        limit=53 * 1024 * 1024,
-    )
-    parts = call(local_kernel, whole, (panel, signs.reshape(BLOCKS, LANES)), "local_transform")
+    in_hbm = lambda value: pltpu.with_memory_space_constraint(value, pltpu.HBM)
+    parts, samples = call(
+        local_kernel,
+        (pltpu.VMEM((1024, LANES), f32), pltpu.VMEM((LANES, LANES), jnp.int32)),
+        (
+            in_hbm(panel),
+            in_hbm(signs.reshape(BLOCKS, LANES)),
+            in_hbm(samples.reshape(LANES, LANES)),
+        ),
+        "local_transform",
+        specs=[HBM] * 3,
+        scratch=[
+            pltpu.VMEM((2, 8, LOCAL_ROWS), f32),
+            pltpu.VMEM((BLOCKS, LANES), jnp.int32),
+            pltpu.SemaphoreType.DMA((4,)),
+        ],
+    )
     parts = exchange(parts.reshape(CHIPS, 8, LANES)).reshape(1024, LANES)
     parts, samples = lax.optimization_barrier((parts, samples))
     other = lax.ppermute(parts, "core", [(0, 1), (1, 0)])
@@ -207,7 +235,7 @@
     counts = call(
         count_kernel,
         jax.ShapeDtypeStruct((2 * BLOCKS, CHIPS), f32),
-        (samples.reshape(LANES, LANES),),
+        (samples,),
         "count_samples",
         flops=1 << 30,
     )
@@ -226,6 +254,12 @@
         ),
         (back,),
         "place_rows",
+        out_specs=(HBM, HBM),
+        scratch=[
+            pltpu.VMEM((2, 8, LOCAL_ROWS), f32),
+            pltpu.VMEM((COLUMNS, COLUMNS), f32),
+            pltpu.SemaphoreType.DMA((3,)),
+        ],
     )
 
 

time: 70.2 us -> 70.1 us (level)
    pallas_call x6 -> x5, Pallas kernels: 5.41 us -> 5.43 us  [call(): pl.pallas_call(kernel, out_shape=outs, in_specs=specs or [VMEM] * len(ope...]
where the time goes in v4:
time: 70.1 us; the launch traced here: 69.4 us
  blocking collectives  60.3 us (86%)
  Pallas kernels  5.43 us (8%)
  starting transfers between devices  2.96 us (4%)
    all_to_all x2, blocking collectives, per_device(): exchange = lambda value: lax.all_to_all(value, CHIP_AXES, 0, 0, tiled=True)  60.3 us
    pallas_call x5, Pallas kernels, call(): pl.pallas_call(kernel, out_shape=outs, in_specs=specs or [VMEM] * len(ope...  5.43 us
    ppermute x1, starting transfers between devices, per_device(): other = lax.ppermute(parts, 'core', [(0, 1), (1, 0)])  2.96 us
  transfers between devices with their start and end apart: 1, of which 0 were waited for; matrix products, arithmetic and copies ran while one was open for 0% of the time, Pallas kernels for 2%

profile of v4, /device:TPU:1, one launch (start us, length us, event | category | flops | bytes accessed | tf_op | source)
XLA Modules:
  0.0 69.4 jit_solution(8530332841774334433)
XLA Ops:
  0.6 1.6 %local_transform.1 = (f32[1024,128]{1,0:T(8,128)S(1)}, s32[128,128]{1,0:T(8,128)S(1)}) custom-call(f32[16,8192]{1,0:T(8,128)} %panel_hbm.1, s32[64,128]{1,0:T(8,128)} %bitcast.12, s32[128,128]{1,0:T(8,128)} %bitcast.11), custom_call_target="tpu_custom_call" | custom-call | bytes 1048576 | tf_op jit(solution)/shard_map/local_transform/pallas_call | solution.py:198
  2.2 33.3 %all_to_all.10 = f32[128,8,128]{2,1,0:T(8,128)S(1)} all-to-all(f32[128,8,128]{2,1,0:T(8,128)S(1)} %bitcast.10), channel_id=1, replica_groups=mesh['wide'=16,'slow'=8,'core'=2] {'wide','slow'}, dimensions={0} | all-to-all | bytes 1048576 | tf_op jit(solution)/shard_map/all_to_all | solution.py:213
  35.5 3.0 %collective-permute-start = (f32[1024,128]{1,0:T(8,128)S(1)}, f32[1024,128]{1,0:T(8,128)S(1)}, u32[]{:S(2)}, u32[]{:S(2)}) collective-permute-start(f32[1024,128]{1,0:T(8,128)S(1)} %bitcast.8), channel_id=1, source_target_pairs={{0,1},{1,0},{2,3},{3,2},{4,5},{5,4},{6,7},{7,6},{8,9},{9,8},{10,11... | collective-permute-start | bytes 1572872 | tf_op jit(solution)/shard_map/ppermute | solution.py:233
  38.5 0.4 own_chips_transform.1
  38.9 1.2 %count_samples.1.count_ref = f32[128,128]{1,0:T(8,128)S(1)} custom-call(s32[128,128]{1,0:T(8,128)S(1)} %get-tuple-element.13.samples_ref), custom_call_target="tpu_custom_call" | custom-call | flops 1073741824 | bytes 1048576 | tf_op jit(solution)/shard_map/count_samples/pallas_call | solution.py:198
  40.1 0.0 collective-permute-done.parts_ref
  40.1 1.2 %both_cores.1 = f32[1280,128]{1,0:T(8,128)S(1)} custom-call(f32[1024,128]{1,0:T(8,128)S(1)} %collective-permute-done.parts_ref, f32[1024,128]{1,0:T(8,128)S(1)} %get-tuple-element.11.own_ref, f32[1024,128]{1,0:T(8,128)S(1)} %get-tuple-element.12.turned_ref, f32[128,128]{1,0:T(8,128)S(1)} %count_samples.1.count_ref), custom_call_target="tpu_custom_call" | custom-call | bytes 1048576 | tf_op jit(solution)/shard_map/both_cores/pallas_call | solution.py:198
  41.4 27.0 %all_to_all.11 = f32[128,1,1280]{2,1,0:T(1,128)S(1)} all-to-all(f32[128,1,1280]{2,1,0:T(1,128)S(1)} %bitcast.7), channel_id=1, replica_groups=mesh['wide'=16,'slow'=8,'core'=2] {'wide','slow'}, dimensions={0} | all-to-all | bytes 1310720 | tf_op jit(solution)/shard_map/all_to_all | solution.py:213
  68.4 1.0 %place_rows.1 = (f32[16,8192]{1,0:T(8,128)}, f32[16,16]{1,0:T(8,128)}) custom-call(f32[1280,128]{1,0:T(8,128)S(1)} %bitcast.6), custom_call_target="tpu_custom_call" | custom-call | bytes 1048576 | tf_op jit(solution)/shard_map/place_rows/pallas_call | solution.py:198
Async XLA Ops:
  35.5 4.6 %collective-permute-start = (f32[1024,128]{1,0:T(8,128)S(1)}, f32[1024,128]{1,0:T(8,128)S(1)}, u32[]{:S(2)}, u32[]{:S(2)}) collective-permute-start(f32[1024,128]{1,0:T(8,128)S(1)} %bitcast.8), channel_id=1, source_target_pairs={{0,1},{1,0},{2,3},{3,2},{4,5},{5,4},{6,7},{7,6},{8,9},{9,8},{10,11... | collective-permute-start | bytes 1572872 | tf_op jit(solution)/shard_map/ppermute | solution.py:233

commit v5 on v4

--- a/solution.py
+++ b/solution.py
@@ -13,11 +13,11 @@
 LOCAL_ROWS = BLOCKS * LANES
 ROWS = 2 * CHIPS * LOCAL_ROWS
 SAMPLES = 16384
+CHUNKS = 8
 WIDTH = 10
 CHIP_AXES = ("wide", "slow")
 ALL_AXES = ("wide", "slow", "core")
 NT = (((1,), (1,)), ((), ()))
-HIGH = lax.Precision.HIGHEST
 VMEM = pl.BlockSpec(memory_space=pltpu.VMEM)
 HBM = pl.BlockSpec(memory_space=pltpu.HBM)
 LIMIT = 32 * 1024 * 1024
@@ -38,6 +38,21 @@
     high = value.astype(jnp.bfloat16)
     low = (value - high.astype(jnp.float32)).astype(jnp.bfloat16)
     return high, low
+
+
+def columns_alike(rows, lanes):
+    first = lax.broadcasted_iota(jnp.int32, (rows, lanes), 0)
+    second = lax.broadcasted_iota(jnp.int32, (rows, lanes), 1)
+    return jnp.where(((first ^ second) & 15) == 0, 1.0, 0.0).astype(jnp.bfloat16)
+
+
+def exact_pick(value, ones):
+    count = value.shape[0]
+    high, low = split(value)
+    rest = value - high.astype(jnp.float32) - low.astype(jnp.float32)
+    parts = jnp.concatenate([high, low, rest.astype(jnp.bfloat16)], axis=0)
+    done = jnp.dot(parts, ones, preferred_element_type=jnp.float32)
+    return done[:count, :] + done[count : 2 * count, :] + done[2 * count :, :]
 
 
 def butterfly(parts):
@@ -143,15 +158,25 @@
             )
     counts = count_ref[...]
     weighed = [column * counts[b : b + 1, :] for b, column in enumerate(columns)]
-    weighed = jnp.concatenate(split(jnp.concatenate(weighed, axis=1)), axis=0)
-    columns = jnp.concatenate(split(jnp.concatenate(columns, axis=1)), axis=0)
-    gram = lax.dot_general(weighed, columns, NT, preferred_element_type=jnp.float32)
-    gram = gram[:, :COLUMNS] + gram[:, COLUMNS:]
+    chunk = 2 * BLOCKS // CHUNKS
+
+    def stacked(values):
+        rows = []
+        for c in range(CHUNKS):
+            rows += split(jnp.concatenate(values[c * chunk : (c + 1) * chunk], axis=1))
+        return jnp.concatenate(rows, axis=0)
+
+    square = lax.dot_general(
+        stacked(weighed), stacked(columns), NT, preferred_element_type=jnp.float32
+    )
+    lane_chunk = lax.broadcasted_iota(jnp.int32, (32, 32 * CHUNKS), 1) >> 5
+    gram = jnp.zeros((32, 32 * CHUNKS), jnp.float32)
+    for c in range(CHUNKS):
+        gram = jnp.where(lane_chunk == c, square[32 * c : 32 * c + 32, :], gram)
     gram = gram[:COLUMNS, :] + gram[COLUMNS:, :]
+    tiled = exact_pick(gram, columns_alike(32 * CHUNKS, LANES))
     lanes = lax.broadcasted_iota(jnp.int32, (COLUMNS, LANES), 1)
     rows = lax.broadcasted_iota(jnp.int32, (COLUMNS, LANES), 0)
-    tile = jnp.where((lanes & 15) == rows, 1.0, 0.0)
-    tiled = jnp.dot(gram, tile, precision=HIGH, preferred_element_type=jnp.float32)
     kept = jnp.where((lanes >> 4) == (rows & 7), tiled, 0.0)
     for half in range(2):
         flat = jnp.sum(kept[8 * half : 8 * half + 8, :], axis=0, keepdims=True)
@@ -159,14 +184,6 @@
 
 
 def place_kernel(parts_ref, out_hbm, gram_hbm, out_ref, gram_ref, sems):
-    lanes = lax.broadcasted_iota(jnp.int32, (8, LANES), 1)
-    rows = lax.broadcasted_iota(jnp.int32, (8, LANES), 0)
-    pick = jnp.where(
-        (lax.broadcasted_iota(jnp.int32, (LANES, COLUMNS), 0) & 15)
-        == lax.broadcasted_iota(jnp.int32, (LANES, COLUMNS), 1),
-        1.0,
-        0.0,
-    )
     copies = []
     for half in range(2):
         for quarter in range(4):
@@ -182,12 +199,15 @@
             )
         )
         copies[half].start()
-        flat = jnp.sum(
-            parts_ref[pl.ds(8 + half, CHIPS, stride=WIDTH), :], axis=0, keepdims=True
-        )
-        spread = jnp.where((lanes >> 4) == rows, jnp.broadcast_to(flat, (8, LANES)), 0.0)
-        block = jnp.dot(spread, pick, precision=HIGH, preferred_element_type=jnp.float32)
-        gram_ref[8 * half : 8 * half + 8, :] = block / jnp.float32(SAMPLES)
+    flat = [
+        jnp.sum(parts_ref[pl.ds(8 + half, CHIPS, stride=WIDTH), :], axis=0, keepdims=True)
+        for half in range(2)
+    ]
+    lanes = lax.broadcasted_iota(jnp.int32, (COLUMNS, LANES), 1)
+    rows = lax.broadcasted_iota(jnp.int32, (COLUMNS, LANES), 0)
+    spread = jnp.where(rows < 8, flat[0], flat[1])
+    spread = jnp.where((lanes >> 4) == (rows & 7), spread, 0.0)
+    gram_ref[...] = exact_pick(spread, columns_alike(LANES, COLUMNS)) / jnp.float32(SAMPLES)
     copies.append(pltpu.make_async_copy(gram_ref, gram_hbm, sems.at[2]))
     copies[2].start()
     for copy in copies:

time: 70.1 us -> 69.9 us (level)
  no operation moved by 1% of the time
where the time goes in v5:
time: 69.9 us; the launch traced here: 69.1 us
  blocking collectives  60.3 us (86%)
  Pallas kernels  5.19 us (7%)
  starting transfers between devices  2.96 us (4%)
    all_to_all x2, blocking collectives, per_device(): exchange = lambda value: lax.all_to_all(value, CHIP_AXES, 0, 0, tiled=True)  60.3 us
    pallas_call x5, Pallas kernels, call(): pl.pallas_call(kernel, out_shape=outs, in_specs=specs or [VMEM] * len(ope...  5.19 us
    ppermute x1, starting transfers between devices, per_device(): other = lax.ppermute(parts, 'core', [(0, 1), (1, 0)])  2.96 us
  transfers between devices with their start and end apart: 1, of which 0 were waited for; matrix products, arithmetic and copies ran while one was open for 0% of the time, Pallas kernels for 2%

profile of v5, /device:TPU:1, one launch (start us, length us, event | category | flops | bytes accessed | tf_op | source)
XLA Modules:
  0.0 69.1 jit_solution(18357265416797157688)
XLA Ops:
  0.6 1.6 %local_transform.1 = (f32[1024,128]{1,0:T(8,128)S(1)}, s32[128,128]{1,0:T(8,128)S(1)}) custom-call(f32[16,8192]{1,0:T(8,128)} %panel_hbm.1, s32[64,128]{1,0:T(8,128)} %bitcast.12, s32[128,128]{1,0:T(8,128)} %bitcast.11), custom_call_target="tpu_custom_call" | custom-call | bytes 1048576 | tf_op jit(solution)/shard_map/local_transform/pallas_call | solution.py:218
  2.2 33.3 %all_to_all.10 = f32[128,8,128]{2,1,0:T(8,128)S(1)} all-to-all(f32[128,8,128]{2,1,0:T(8,128)S(1)} %bitcast.10), channel_id=1, replica_groups=mesh['wide'=16,'slow'=8,'core'=2] {'wide','slow'}, dimensions={0} | all-to-all | bytes 1048576 | tf_op jit(solution)/shard_map/all_to_all | solution.py:233
  35.5 3.0 %collective-permute-start = (f32[1024,128]{1,0:T(8,128)S(1)}, f32[1024,128]{1,0:T(8,128)S(1)}, u32[]{:S(2)}, u32[]{:S(2)}) collective-permute-start(f32[1024,128]{1,0:T(8,128)S(1)} %bitcast.8), channel_id=1, source_target_pairs={{0,1},{1,0},{2,3},{3,2},{4,5},{5,4},{6,7},{7,6},{8,9},{9,8},{10,11... | collective-permute-start | bytes 1572872 | tf_op jit(solution)/shard_map/ppermute | solution.py:253
  38.5 0.4 own_chips_transform.1
  38.9 1.2 %count_samples.1.count_ref = f32[128,128]{1,0:T(8,128)S(1)} custom-call(s32[128,128]{1,0:T(8,128)S(1)} %get-tuple-element.13.samples_ref), custom_call_target="tpu_custom_call" | custom-call | flops 1073741824 | bytes 1048576 | tf_op jit(solution)/shard_map/count_samples/pallas_call | solution.py:218
  40.1 0.0 collective-permute-done.parts_ref
  40.1 1.0 %both_cores.1 = f32[1280,128]{1,0:T(8,128)S(1)} custom-call(f32[1024,128]{1,0:T(8,128)S(1)} %collective-permute-done.parts_ref, f32[1024,128]{1,0:T(8,128)S(1)} %get-tuple-element.11.own_ref, f32[1024,128]{1,0:T(8,128)S(1)} %get-tuple-element.12.turned_ref, f32[128,128]{1,0:T(8,128)S(1)} %count_samples.1.count_ref), custom_call_target="tpu_custom_call" | custom-call | bytes 1048576 | tf_op jit(solution)/shard_map/both_cores/pallas_call | solution.py:218
  41.2 27.0 %all_to_all.11 = f32[128,1,1280]{2,1,0:T(1,128)S(1)} all-to-all(f32[128,1,1280]{2,1,0:T(1,128)S(1)} %bitcast.7), channel_id=1, replica_groups=mesh['wide'=16,'slow'=8,'core'=2] {'wide','slow'}, dimensions={0} | all-to-all | bytes 1310720 | tf_op jit(solution)/shard_map/all_to_all | solution.py:233
  68.2 1.0 %place_rows.1 = (f32[16,8192]{1,0:T(8,128)}, f32[16,16]{1,0:T(8,128)}) custom-call(f32[1280,128]{1,0:T(8,128)S(1)} %bitcast.6), custom_call_target="tpu_custom_call" | custom-call | bytes 1048576 | tf_op jit(solution)/shard_map/place_rows/pallas_call | solution.py:218
Async XLA Ops:
  35.5 4.6 %collective-permute-start = (f32[1024,128]{1,0:T(8,128)S(1)}, f32[1024,128]{1,0:T(8,128)S(1)}, u32[]{:S(2)}, u32[]{:S(2)}) collective-permute-start(f32[1024,128]{1,0:T(8,128)S(1)} %bitcast.8), channel_id=1, source_target_pairs={{0,1},{1,0},{2,3},{3,2},{4,5},{5,4},{6,7},{7,6},{8,9},{9,8},{10,11... | collective-permute-start | bytes 1572872 | tf_op jit(solution)/shard_map/ppermute | solution.py:253

commit v6 on v5

--- a/solution.py
+++ b/solution.py
@@ -69,25 +69,20 @@
 def local_kernel(
     panel_hbm, signs_hbm, samples_hbm, out_ref, samples_ref, panel_ref, signs_ref, sems
 ):
-    signs_copy = pltpu.make_async_copy(signs_hbm, signs_ref, sems.at[2])
-    signs_copy.start()
-    halves = []
+    copies = [
+        pltpu.make_async_copy(signs_hbm, signs_ref, sems.at[0]),
+        pltpu.make_async_copy(panel_hbm, panel_ref, sems.at[1]),
+        pltpu.make_async_copy(samples_hbm, samples_ref, sems.at[2]),
+    ]
+    for copy in copies:
+        copy.start()
+    twice = hadamard_twice()
+    copies[0].wait()
+    copies[1].wait()
     for half in range(2):
-        halves.append(
-            pltpu.make_async_copy(
-                panel_hbm.at[pl.ds(8 * half, 8), :], panel_ref.at[half], sems.at[half]
-            )
-        )
-        halves[half].start()
-    samples_copy = pltpu.make_async_copy(samples_hbm, samples_ref, sems.at[3])
-    samples_copy.start()
-    twice = hadamard_twice()
-    signs_copy.wait()
-    for half in range(2):
-        halves[half].wait()
         signs = signs_ref[...].astype(jnp.float32)
         parts = [
-            panel_ref[half, :, b * LANES : (b + 1) * LANES] * signs[b : b + 1, :]
+            panel_ref[8 * half : 8 * half + 8, b * LANES : (b + 1) * LANES] * signs[b : b + 1, :]
             for b in range(BLOCKS)
         ]
         parts = butterfly(parts)
@@ -96,7 +91,7 @@
             pair = jnp.concatenate(split(block), axis=1)
             done = lax.dot_general(twice, pair, NT, preferred_element_type=jnp.float32)
             out_ref[pl.ds(4 * half + quarter, LANES, stride=8), :] = done
-    samples_copy.wait()
+    copies[2].wait()
 
 
 def count_kernel(samples_ref, count_ref):
@@ -193,12 +188,16 @@
                 out_ref[half, :, block * LANES : (block + 1) * LANES] = turned[
                     8 * b : 8 * b + 8, :
                 ]
-        copies.append(
-            pltpu.make_async_copy(
-                out_ref.at[half], out_hbm.at[pl.ds(8 * half, 8), :], sems.at[half]
-            )
-        )
-        copies[half].start()
+            if quarter % 2 == 1:
+                lanes = pl.ds((quarter - 1) * 16 * LANES, 32 * LANES)
+                copies.append(
+                    pltpu.make_async_copy(
+                        out_ref.at[half, :, lanes],
+                        out_hbm.at[pl.ds(8 * half, 8), lanes],
+                        sems.at[len(copies)],
+                    )
+                )
+                copies[-1].start()
     flat = [
         jnp.sum(parts_ref[pl.ds(8 + half, CHIPS, stride=WIDTH), :], axis=0, keepdims=True)
         for half in range(2)
@@ -208,8 +207,8 @@
     spread = jnp.where(rows < 8, flat[0], flat[1])
     spread = jnp.where((lanes >> 4) == (rows & 7), spread, 0.0)
     gram_ref[...] = exact_pick(spread, columns_alike(LANES, COLUMNS)) / jnp.float32(SAMPLES)
-    copies.append(pltpu.make_async_copy(gram_ref, gram_hbm, sems.at[2]))
-    copies[2].start()
+    copies.append(pltpu.make_async_copy(gram_ref, gram_hbm, sems.at[4]))
+    copies[-1].start()
     for copy in copies:
         copy.wait()
 
@@ -243,9 +242,9 @@
         "local_transform",
         specs=[HBM] * 3,
         scratch=[
-            pltpu.VMEM((2, 8, LOCAL_ROWS), f32),
+            pltpu.VMEM((COLUMNS, LOCAL_ROWS), f32),
             pltpu.VMEM((BLOCKS, LANES), jnp.int32),
-            pltpu.SemaphoreType.DMA((4,)),
+            pltpu.SemaphoreType.DMA((3,)),
         ],
     )
     parts = exchange(parts.reshape(CHIPS, 8, LANES)).reshape(1024, LANES)
@@ -278,7 +277,7 @@
         scratch=[
             pltpu.VMEM((2, 8, LOCAL_ROWS), f32),
             pltpu.VMEM((COLUMNS, COLUMNS), f32),
-            pltpu.SemaphoreType.DMA((3,)),
+            pltpu.SemaphoreType.DMA((5,)),
         ],
     )
 

time: 69.9 us -> 69.8 us (level)
  no operation moved by 1% of the time
where the time goes in v6:
time: 69.8 us; the launch traced here: 69 us
  blocking collectives  60.3 us (86%)
  Pallas kernels  5.09 us (7%)
  starting transfers between devices  2.96 us (4%)
    all_to_all x2, blocking collectives, per_device(): exchange = lambda value: lax.all_to_all(value, CHIP_AXES, 0, 0, tiled=True)  60.3 us
    pallas_call x5, Pallas kernels, call(): pl.pallas_call(kernel, out_shape=outs, in_specs=specs or [VMEM] * len(ope...  5.09 us
    ppermute x1, starting transfers between devices, per_device(): other = lax.ppermute(parts, 'core', [(0, 1), (1, 0)])  2.96 us
  transfers between devices with their start and end apart: 1, of which 0 were waited for; matrix products, arithmetic and copies ran while one was open for 0% of the time, Pallas kernels for 2%

profile of v6, /device:TPU:1, one launch (start us, length us, event | category | flops | bytes accessed | tf_op | source)
XLA Modules:
  0.0 69.0 jit_solution(8418570048373724071)
XLA Ops:
  0.6 1.5 %local_transform.1 = (f32[1024,128]{1,0:T(8,128)S(1)}, s32[128,128]{1,0:T(8,128)S(1)}) custom-call(f32[16,8192]{1,0:T(8,128)} %panel_hbm.1, s32[64,128]{1,0:T(8,128)} %bitcast.12, s32[128,128]{1,0:T(8,128)} %bitcast.11), custom_call_target="tpu_custom_call" | custom-call | bytes 1048576 | tf_op jit(solution)/shard_map/local_transform/pallas_call | solution.py:217
  2.2 33.3 %all_to_all.10 = f32[128,8,128]{2,1,0:T(8,128)S(1)} all-to-all(f32[128,8,128]{2,1,0:T(8,128)S(1)} %bitcast.10), channel_id=1, replica_groups=mesh['wide'=16,'slow'=8,'core'=2] {'wide','slow'}, dimensions={0} | all-to-all | bytes 1048576 | tf_op jit(solution)/shard_map/all_to_all | solution.py:232
  35.5 3.0 %collective-permute-start = (f32[1024,128]{1,0:T(8,128)S(1)}, f32[1024,128]{1,0:T(8,128)S(1)}, u32[]{:S(2)}, u32[]{:S(2)}) collective-permute-start(f32[1024,128]{1,0:T(8,128)S(1)} %bitcast.8), channel_id=1, source_target_pairs={{0,1},{1,0},{2,3},{3,2},{4,5},{5,4},{6,7},{7,6},{8,9},{9,8},{10,11... | collective-permute-start | bytes 1572872 | tf_op jit(solution)/shard_map/ppermute | solution.py:252
  38.4 0.4 own_chips_transform.1
  38.8 1.2 %count_samples.1.count_ref = f32[128,128]{1,0:T(8,128)S(1)} custom-call(s32[128,128]{1,0:T(8,128)S(1)} %get-tuple-element.13.samples_ref), custom_call_target="tpu_custom_call" | custom-call | flops 1073741824 | bytes 1048576 | tf_op jit(solution)/shard_map/count_samples/pallas_call | solution.py:217
  40.1 0.0 collective-permute-done.parts_ref
  40.1 1.0 %both_cores.1 = f32[1280,128]{1,0:T(8,128)S(1)} custom-call(f32[1024,128]{1,0:T(8,128)S(1)} %collective-permute-done.parts_ref, f32[1024,128]{1,0:T(8,128)S(1)} %get-tuple-element.11.own_ref, f32[1024,128]{1,0:T(8,128)S(1)} %get-tuple-element.12.turned_ref, f32[128,128]{1,0:T(8,128)S(1)} %count_samples.1.count_ref), custom_call_target="tpu_custom_call" | custom-call | bytes 1048576 | tf_op jit(solution)/shard_map/both_cores/pallas_call | solution.py:217
  41.1 27.0 %all_to_all.11 = f32[128,1,1280]{2,1,0:T(1,128)S(1)} all-to-all(f32[128,1,1280]{2,1,0:T(1,128)S(1)} %bitcast.7), channel_id=1, replica_groups=mesh['wide'=16,'slow'=8,'core'=2] {'wide','slow'}, dimensions={0} | all-to-all | bytes 1310720 | tf_op jit(solution)/shard_map/all_to_all | solution.py:232
  68.1 0.9 %place_rows.1 = (f32[16,8192]{1,0:T(8,128)}, f32[16,16]{1,0:T(8,128)}) custom-call(f32[1280,128]{1,0:T(8,128)S(1)} %bitcast.6), custom_call_target="tpu_custom_call" | custom-call | bytes 1048576 | tf_op jit(solution)/shard_map/place_rows/pallas_call | solution.py:217
Async XLA Ops:
  35.5 4.6 %collective-permute-start = (f32[1024,128]{1,0:T(8,128)S(1)}, f32[1024,128]{1,0:T(8,128)S(1)}, u32[]{:S(2)}, u32[]{:S(2)}) collective-permute-start(f32[1024,128]{1,0:T(8,128)S(1)} %bitcast.8), channel_id=1, source_target_pairs={{0,1},{1,0},{2,3},{3,2},{4,5},{5,4},{6,7},{7,6},{8,9},{9,8},{10,11... | collective-permute-start | bytes 1572872 | tf_op jit(solution)/shard_map/ppermute | solution.py:252

commit v7 on v6

--- a/solution.py
+++ b/solution.py
@@ -15,7 +15,8 @@
 SAMPLES = 16384
 CHUNKS = 8
 WIDTH = 10
-CHIP_AXES = ("wide", "slow")
+OUT_AXES = ("wide", "slow")
+BACK_AXES = ("slow", "wide")
 ALL_AXES = ("wide", "slow", "core")
 NT = (((1,), (1,)), ((), ()))
 VMEM = pl.BlockSpec(memory_space=pltpu.VMEM)
@@ -23,8 +24,16 @@
 LIMIT = 32 * 1024 * 1024
 
 
-def hadamard_twice():
-    first = lax.broadcasted_iota(jnp.int32, (LANES, LANES), 0)
+def there(chip):
+    return ((chip & 7) << 4) | (chip >> 3)
+
+
+def back_again(chip):
+    return ((chip & 15) << 3) | (chip >> 4)
+
+
+def hadamard_twice(row_of):
+    first = row_of(lax.broadcasted_iota(jnp.int32, (LANES, LANES), 0))
     second = lax.broadcasted_iota(jnp.int32, (LANES, LANES), 1)
     bits = first & second
     bits = bits ^ (bits >> 4)
@@ -76,7 +85,7 @@
     ]
     for copy in copies:
         copy.start()
-    twice = hadamard_twice()
+    twice = hadamard_twice(there)
     copies[0].wait()
     copies[1].wait()
     for half in range(2):
@@ -95,11 +104,11 @@
 
 
 def count_kernel(samples_ref, count_ref):
-    chip = lax.axis_index("wide") * lax.axis_size("slow") + lax.axis_index("slow")
+    chip = lax.axis_index("slow") * lax.axis_size("wide") + lax.axis_index("wide")
     rows = samples_ref[...]
     place = ((rows >> 13) & 1) * BLOCKS + ((rows >> 7) & 63)
     place = jnp.where((rows & 127) == chip, place, -1).astype(jnp.float32)
-    owner = (rows >> 14).astype(jnp.float32)
+    owner = there(rows >> 14).astype(jnp.float32)
     index = lax.broadcasted_iota(jnp.int32, (CHIPS, LANES), 0)
     index = index.astype(jnp.float32).astype(jnp.bfloat16)
     one, zero = jnp.ones_like(index), jnp.zeros_like(index)
@@ -123,7 +132,7 @@
 
 def own_kernel(parts_ref, out_ref, turned_ref):
     scale = 1.0 / jnp.sqrt(jnp.float32(ROWS))
-    twice = hadamard_twice()
+    twice = hadamard_twice(back_again)
     for group in range(8):
         done = chips_transform(parts_ref, group, twice)
         rows = slice(group * CHIPS, (group + 1) * CHIPS)
@@ -135,7 +144,7 @@
 def both_kernel(parts_ref, own_ref, turned_ref, count_ref, out_ref):
     scale = 1.0 / jnp.sqrt(jnp.float32(ROWS))
     side = (1 - 2 * lax.axis_index("core")).astype(jnp.float32)
-    twice = hadamard_twice()
+    twice = hadamard_twice(back_again)
     sums, gaps = [], []
     for group in range(8):
         done = chips_transform(parts_ref, group, twice) * scale
@@ -229,7 +238,7 @@
 def per_device(panel, signs, samples):
     f32 = jnp.float32
     whole = jax.ShapeDtypeStruct((1024, LANES), f32)
-    exchange = lambda value: lax.all_to_all(value, CHIP_AXES, 0, 0, tiled=True)
+    exchange = lambda value, axes: lax.all_to_all(value, axes, 0, 0, tiled=True)
     in_hbm = lambda value: pltpu.with_memory_space_constraint(value, pltpu.HBM)
     parts, samples = call(
         local_kernel,
@@ -247,7 +256,7 @@
             pltpu.SemaphoreType.DMA((3,)),
         ],
     )
-    parts = exchange(parts.reshape(CHIPS, 8, LANES)).reshape(1024, LANES)
+    parts = exchange(parts.reshape(CHIPS, 8, LANES), OUT_AXES).reshape(1024, LANES)
     parts, samples = lax.optimization_barrier((parts, samples))
     other = lax.ppermute(parts, "core", [(0, 1), (1, 0)])
     own, turned = call(own_kernel, (whole, whole), (parts,), "own_chips_transform", flops=1 << 28)
@@ -264,7 +273,8 @@
         (other, own, turned, counts),
         "both_cores",
     )
-    back = exchange(back.reshape(CHIPS, 1, WIDTH * LANES)).reshape(CHIPS * WIDTH, LANES)
+    back = exchange(back.reshape(CHIPS, 1, WIDTH * LANES), BACK_AXES)
+    back = back.reshape(CHIPS * WIDTH, LANES)
     return call(
         place_kernel,
         (

time: 69.8 us -> 69 us (0.989)
  no operation moved by 1% of the time
where the time goes in v7:
time: 69 us; the launch traced here: 68.6 us
  blocking collectives  59.8 us (87%)
  Pallas kernels  5.13 us (7%)
  starting transfers between devices  2.96 us (4%)
    all_to_all x2, blocking collectives, per_device(): exchange = lambda value, axes: lax.all_to_all(value, axes, 0, 0, tiled=True)  59.8 us
    pallas_call x5, Pallas kernels, call(): pl.pallas_call(kernel, out_shape=outs, in_specs=specs or [VMEM] * len(ope...  5.13 us
    ppermute x1, starting transfers between devices, per_device(): other = lax.ppermute(parts, 'core', [(0, 1), (1, 0)])  2.96 us
  transfers between devices with their start and end apart: 1, of which 0 were waited for; matrix products, arithmetic and copies ran while one was open for 0% of the time, Pallas kernels for 2%

profile of v7, /device:TPU:1, one launch (start us, length us, event | category | flops | bytes accessed | tf_op | source)
XLA Modules:
  0.0 68.6 jit_solution(1681706066146507640)
XLA Ops:
  0.6 1.5 %local_transform.1 = (f32[1024,128]{1,0:T(8,128)S(1)}, s32[128,128]{1,0:T(8,128)S(1)}) custom-call(f32[16,8192]{1,0:T(8,128)} %panel_hbm.1, s32[64,128]{1,0:T(8,128)} %bitcast.12, s32[128,128]{1,0:T(8,128)} %bitcast.11), custom_call_target="tpu_custom_call" | custom-call | bytes 1048576 | tf_op jit(solution)/shard_map/local_transform/pallas_call | solution.py:226
  2.2 33.3 %all_to_all.10 = f32[128,8,128]{2,1,0:T(8,128)S(1)} all-to-all(f32[128,8,128]{2,1,0:T(8,128)S(1)} %bitcast.10), channel_id=1, replica_groups=mesh['wide'=16,'slow'=8,'core'=2] {'wide','slow'}, dimensions={0} | all-to-all | bytes 1048576 | tf_op jit(solution)/shard_map/all_to_all | solution.py:241
  35.5 3.0 %collective-permute-start = (f32[1024,128]{1,0:T(8,128)S(1)}, f32[1024,128]{1,0:T(8,128)S(1)}, u32[]{:S(2)}, u32[]{:S(2)}) collective-permute-start(f32[1024,128]{1,0:T(8,128)S(1)} %bitcast.8), channel_id=1, source_target_pairs={{0,1},{1,0},{2,3},{3,2},{4,5},{5,4},{6,7},{7,6},{8,9},{9,8},{10,11... | collective-permute-start | bytes 1572872 | tf_op jit(solution)/shard_map/ppermute | solution.py:261
  38.4 0.4 own_chips_transform.1
  38.8 1.2 %count_samples.1.count_ref = f32[128,128]{1,0:T(8,128)S(1)} custom-call(s32[128,128]{1,0:T(8,128)S(1)} %get-tuple-element.13.samples_ref), custom_call_target="tpu_custom_call" | custom-call | flops 1073741824 | bytes 1048576 | tf_op jit(solution)/shard_map/count_samples/pallas_call | solution.py:226
  40.1 0.0 collective-permute-done.parts_ref
  40.1 1.0 %both_cores.1 = f32[1280,128]{1,0:T(8,128)S(1)} custom-call(f32[1024,128]{1,0:T(8,128)S(1)} %collective-permute-done.parts_ref, f32[1024,128]{1,0:T(8,128)S(1)} %get-tuple-element.11.own_ref, f32[1024,128]{1,0:T(8,128)S(1)} %get-tuple-element.12.turned_ref, f32[128,128]{1,0:T(8,128)S(1)} %count_samples.1.count_ref), custom_call_target="tpu_custom_call" | custom-call | bytes 1048576 | tf_op jit(solution)/shard_map/both_cores/pallas_call | solution.py:226
  41.1 26.5 %all_to_all.11 = f32[128,1,1280]{2,1,0:T(1,128)S(1)} all-to-all(f32[128,1,1280]{2,1,0:T(1,128)S(1)} %bitcast.7), channel_id=1, replica_groups=mesh['wide'=16,'slow'=8,'core'=2] {'slow','wide'}, dimensions={0} | all-to-all | bytes 1310720 | tf_op jit(solution)/shard_map/all_to_all | solution.py:241
  67.7 0.9 %place_rows.1 = (f32[16,8192]{1,0:T(8,128)}, f32[16,16]{1,0:T(8,128)}) custom-call(f32[1280,128]{1,0:T(8,128)S(1)} %bitcast.6), custom_call_target="tpu_custom_call" | custom-call | bytes 1048576 | tf_op jit(solution)/shard_map/place_rows/pallas_call | solution.py:226
Async XLA Ops:
  35.5 4.6 %collective-permute-start = (f32[1024,128]{1,0:T(8,128)S(1)}, f32[1024,128]{1,0:T(8,128)S(1)}, u32[]{:S(2)}, u32[]{:S(2)}) collective-permute-start(f32[1024,128]{1,0:T(8,128)S(1)} %bitcast.8), channel_id=1, source_target_pairs={{0,1},{1,0},{2,3},{3,2},{4,5},{5,4},{6,7},{7,6},{8,9},{9,8},{10,11... | collective-permute-start | bytes 1572872 | tf_op jit(solution)/shard_map/ppermute | solution.py:261

commit v8 on v7

--- a/solution.py
+++ b/solution.py
@@ -139,6 +139,11 @@
         done = done * scale
         out_ref[rows, :] = done
         turned_ref[rows, :] = done.T
+
+
+def beside_kernel(parts_ref, samples_ref, out_ref, turned_ref, count_ref):
+    own_kernel(parts_ref, out_ref, turned_ref)
+    count_kernel(samples_ref, count_ref)
 
 
 def both_kernel(parts_ref, own_ref, turned_ref, count_ref, out_ref):
@@ -259,12 +264,11 @@
     parts = exchange(parts.reshape(CHIPS, 8, LANES), OUT_AXES).reshape(1024, LANES)
     parts, samples = lax.optimization_barrier((parts, samples))
     other = lax.ppermute(parts, "core", [(0, 1), (1, 0)])
-    own, turned = call(own_kernel, (whole, whole), (parts,), "own_chips_transform", flops=1 << 28)
-    counts = call(
-        count_kernel,
-        jax.ShapeDtypeStruct((2 * BLOCKS, CHIPS), f32),
-        (samples,),
-        "count_samples",
+    own, turned, counts = call(
+        beside_kernel,
+        (whole, whole, jax.ShapeDtypeStruct((2 * BLOCKS, CHIPS), f32)),
+        (parts, samples),
+        "own_and_counts",
         flops=1 << 30,
     )
     back = call(

time: 69 us -> 68.9 us (level)
    pallas_call x5 -> x4, Pallas kernels: 5.13 us -> 4.91 us  [call(): pl.pallas_call(kernel, out_shape=outs, in_specs=specs or [VMEM] * len(ope...]
  transfers between devices with their start and end apart: 1 -> 1, of which waited for: 0 -> 1; matrix products, arithmetic and copies ran while one was open for 0% -> 0% of each run, Pallas kernels for 2% -> 2%
where the time goes in v8:
time: 68.9 us; the launch traced here: 68.4 us
  blocking collectives  59.7 us (87%)
  Pallas kernels  4.91 us (7%)
  starting transfers between devices  2.96 us (4%)
    all_to_all x2, blocking collectives, per_device(): exchange = lambda value, axes: lax.all_to_all(value, axes, 0, 0, tiled=True)  59.7 us
    pallas_call x4, Pallas kernels, call(): pl.pallas_call(kernel, out_shape=outs, in_specs=specs or [VMEM] * len(ope...  4.91 us
    ppermute x1, starting transfers between devices, per_device(): other = lax.ppermute(parts, 'core', [(0, 1), (1, 0)])  2.96 us
  transfers between devices with their start and end apart: 1, of which 1 were waited for; matrix products, arithmetic and copies ran while one was open for 0% of the time, Pallas kernels for 2%

profile of v8, /device:TPU:1, one launch (start us, length us, event | category | flops | bytes accessed | tf_op | source)
XLA Modules:
  0.0 68.4 jit_solution(1772756101664865258)
XLA Ops:
  0.6 1.5 %local_transform.1 = (f32[1024,128]{1,0:T(8,128)S(1)}, s32[128,128]{1,0:T(8,128)S(1)}) custom-call(f32[16,8192]{1,0:T(8,128)} %panel_hbm.1, s32[64,128]{1,0:T(8,128)} %bitcast.12, s32[128,128]{1,0:T(8,128)} %bitcast.11), custom_call_target="tpu_custom_call" | custom-call | bytes 1048576 | tf_op jit(solution)/shard_map/local_transform/pallas_call | solution.py:231
  2.2 33.3 %all_to_all.10 = f32[128,8,128]{2,1,0:T(8,128)S(1)} all-to-all(f32[128,8,128]{2,1,0:T(8,128)S(1)} %bitcast.10), channel_id=1, replica_groups=mesh['wide'=16,'slow'=8,'core'=2] {'wide','slow'}, dimensions={0} | all-to-all | bytes 1048576 | tf_op jit(solution)/shard_map/all_to_all | solution.py:246
  35.5 3.0 %collective-permute-start = (f32[1024,128]{1,0:T(8,128)S(1)}, f32[1024,128]{1,0:T(8,128)S(1)}, u32[]{:S(2)}, u32[]{:S(2)}) collective-permute-start(f32[1024,128]{1,0:T(8,128)S(1)} %bitcast.8), channel_id=1, source_target_pairs={{0,1},{1,0},{2,3},{3,2},{4,5},{5,4},{6,7},{7,6},{8,9},{9,8},{10,11... | collective-permute-start | bytes 1572872 | tf_op jit(solution)/shard_map/ppermute | solution.py:266
  38.4 1.4 %own_and_counts.1 = (f32[1024,128]{1,0:T(8,128)S(1)}, f32[1024,128]{1,0:T(8,128)S(1)}, f32[128,128]{1,0:T(8,128)S(1)}) custom-call(f32[1024,128]{1,0:T(8,128)S(1)} %bitcast.9, s32[128,128]{1,0:T(8,128)S(1)} %get-tuple-element.12.samples_ref), custom_call_target="tpu_custom_call" | custom-call | flops 1073741824 | bytes 1048576 | tf_op jit(solution)/shard_map/own_and_counts/pallas_call | solution.py:231
  39.8 0.1 collective-permute-done.parts_ref
  39.9 1.0 %both_cores.1 = f32[1280,128]{1,0:T(8,128)S(1)} custom-call(f32[1024,128]{1,0:T(8,128)S(1)} %collective-permute-done.parts_ref, f32[1024,128]{1,0:T(8,128)S(1)} %get-tuple-element.13.own_ref, f32[1024,128]{1,0:T(8,128)S(1)} %get-tuple-element.14.turned_ref, f32[128,128]{1,0:T(8,128)S(1)} %get-tuple-element.15.count_ref), custom_call_target="tpu_custom_call" | custom-call | bytes 1048576 | tf_op jit(solution)/shard_map/both_cores/pallas_call | solution.py:231
  41.0 26.4 %all_to_all.11 = f32[128,1,1280]{2,1,0:T(1,128)S(1)} all-to-all(f32[128,1,1280]{2,1,0:T(1,128)S(1)} %bitcast.7), channel_id=1, replica_groups=mesh['wide'=16,'slow'=8,'core'=2] {'slow','wide'}, dimensions={0} | all-to-all | bytes 1310720 | tf_op jit(solution)/shard_map/all_to_all | solution.py:246
  67.4 0.9 %place_rows.1 = (f32[16,8192]{1,0:T(8,128)}, f32[16,16]{1,0:T(8,128)}) custom-call(f32[1280,128]{1,0:T(8,128)S(1)} %bitcast.6), custom_call_target="tpu_custom_call" | custom-call | bytes 1048576 | tf_op jit(solution)/shard_map/place_rows/pallas_call | solution.py:231
Async XLA Ops:
  35.5 4.5 %collective-permute-start = (f32[1024,128]{1,0:T(8,128)S(1)}, f32[1024,128]{1,0:T(8,128)S(1)}, u32[]{:S(2)}, u32[]{:S(2)}) collective-permute-start(f32[1024,128]{1,0:T(8,128)S(1)} %bitcast.8), channel_id=1, source_target_pairs={{0,1},{1,0},{2,3},{3,2},{4,5},{5,4},{6,7},{7,6},{8,9},{9,8},{10,11... | collective-permute-start | bytes 1572872 | tf_op jit(solution)/shard_map/ppermute | solution.py:266

commit v9 on v8

--- a/solution.py
+++ b/solution.py
@@ -83,8 +83,8 @@
         pltpu.make_async_copy(panel_hbm, panel_ref, sems.at[1]),
         pltpu.make_async_copy(samples_hbm, samples_ref, sems.at[2]),
     ]
-    for copy in copies:
-        copy.start()
+    for index in (1, 0, 2):
+        copies[index].start()
     twice = hadamard_twice(there)
     copies[0].wait()
     copies[1].wait()

time: 68.9 us -> 68.9 us (level)
  no operation moved by 1% of the time
where the time goes in v9:
time: 68.9 us; the launch traced here: 68.3 us
  blocking collectives  59.7 us (87%)
  Pallas kernels  4.88 us (7%)
  starting transfers between devices  2.96 us (4%)
    all_to_all x2, blocking collectives, per_device(): exchange = lambda value, axes: lax.all_to_all(value, axes, 0, 0, tiled=True)  59.7 us
    pallas_call x4, Pallas kernels, call(): pl.pallas_call(kernel, out_shape=outs, in_specs=specs or [VMEM] * len(ope...  4.88 us
    ppermute x1, starting transfers between devices, per_device(): other = lax.ppermute(parts, 'core', [(0, 1), (1, 0)])  2.96 us
  transfers between devices with their start and end apart: 1, of which 1 were waited for; matrix products, arithmetic and copies ran while one was open for 0% of the time, Pallas kernels for 2%

profile of v9, /device:TPU:1, one launch (start us, length us, event | category | flops | bytes accessed | tf_op | source)
XLA Modules:
  0.0 68.3 jit_solution(17528281243498381117)
XLA Ops:
  0.6 1.5 %local_transform.1 = (f32[1024,128]{1,0:T(8,128)S(1)}, s32[128,128]{1,0:T(8,128)S(1)}) custom-call(f32[16,8192]{1,0:T(8,128)} %panel_hbm.1, s32[64,128]{1,0:T(8,128)} %bitcast.12, s32[128,128]{1,0:T(8,128)} %bitcast.11), custom_call_target="tpu_custom_call" | custom-call | bytes 1048576 | tf_op jit(solution)/shard_map/local_transform/pallas_call | solution.py:231
  2.1 33.3 %all_to_all.10 = f32[128,8,128]{2,1,0:T(8,128)S(1)} all-to-all(f32[128,8,128]{2,1,0:T(8,128)S(1)} %bitcast.10), channel_id=1, replica_groups=mesh['wide'=16,'slow'=8,'core'=2] {'wide','slow'}, dimensions={0} | all-to-all | bytes 1048576 | tf_op jit(solution)/shard_map/all_to_all | solution.py:246
  35.4 3.0 %collective-permute-start = (f32[1024,128]{1,0:T(8,128)S(1)}, f32[1024,128]{1,0:T(8,128)S(1)}, u32[]{:S(2)}, u32[]{:S(2)}) collective-permute-start(f32[1024,128]{1,0:T(8,128)S(1)} %bitcast.8), channel_id=1, source_target_pairs={{0,1},{1,0},{2,3},{3,2},{4,5},{5,4},{6,7},{7,6},{8,9},{9,8},{10,11... | collective-permute-start | bytes 1572872 | tf_op jit(solution)/shard_map/ppermute | solution.py:266
  38.4 1.4 %own_and_counts.1 = (f32[1024,128]{1,0:T(8,128)S(1)}, f32[1024,128]{1,0:T(8,128)S(1)}, f32[128,128]{1,0:T(8,128)S(1)}) custom-call(f32[1024,128]{1,0:T(8,128)S(1)} %bitcast.9, s32[128,128]{1,0:T(8,128)S(1)} %get-tuple-element.12.samples_ref), custom_call_target="tpu_custom_call" | custom-call | flops 1073741824 | bytes 1048576 | tf_op jit(solution)/shard_map/own_and_counts/pallas_call | solution.py:231
  39.8 0.1 collective-permute-done.parts_ref
  39.9 1.0 %both_cores.1 = f32[1280,128]{1,0:T(8,128)S(1)} custom-call(f32[1024,128]{1,0:T(8,128)S(1)} %collective-permute-done.parts_ref, f32[1024,128]{1,0:T(8,128)S(1)} %get-tuple-element.13.own_ref, f32[1024,128]{1,0:T(8,128)S(1)} %get-tuple-element.14.turned_ref, f32[128,128]{1,0:T(8,128)S(1)} %get-tuple-element.15.count_ref), custom_call_target="tpu_custom_call" | custom-call | bytes 1048576 | tf_op jit(solution)/shard_map/both_cores/pallas_call | solution.py:231
  41.0 26.4 %all_to_all.11 = f32[128,1,1280]{2,1,0:T(1,128)S(1)} all-to-all(f32[128,1,1280]{2,1,0:T(1,128)S(1)} %bitcast.7), channel_id=1, replica_groups=mesh['wide'=16,'slow'=8,'core'=2] {'slow','wide'}, dimensions={0} | all-to-all | bytes 1310720 | tf_op jit(solution)/shard_map/all_to_all | solution.py:246
  67.4 0.9 %place_rows.1 = (f32[16,8192]{1,0:T(8,128)}, f32[16,16]{1,0:T(8,128)}) custom-call(f32[1280,128]{1,0:T(8,128)S(1)} %bitcast.6), custom_call_target="tpu_custom_call" | custom-call | bytes 1048576 | tf_op jit(solution)/shard_map/place_rows/pallas_call | solution.py:231
Async XLA Ops:
  35.4 4.5 %collective-permute-start = (f32[1024,128]{1,0:T(8,128)S(1)}, f32[1024,128]{1,0:T(8,128)S(1)}, u32[]{:S(2)}, u32[]{:S(2)}) collective-permute-start(f32[1024,128]{1,0:T(8,128)S(1)} %bitcast.8), channel_id=1, source_target_pairs={{0,1},{1,0},{2,3},{3,2},{4,5},{5,4},{6,7},{7,6},{8,9},{9,8},{10,11... | collective-permute-start | bytes 1572872 | tf_op jit(solution)/shard_map/ppermute | solution.py:266
